TPU v7x, 128 devices: a whole 4x4x4 slice. The times are simulated.
128 devices in a mesh: panel: 32 (over y, x, core), lag: 4 (over z).
Axes of the slice: x: 4, y: 4, z: 4, core: 2. Of those that a mesh axis runs over, the one named last changes fastest.
Arguments:
- strengths: bfloat16 [131072, 384], P(('panel', 'lag')), may hold values from -6 to 6
- incident_green: bfloat16 [32768, 128, 128], P(('panel', 'lag')), may hold values from -0.02734375 to 0.02734375
- targets: int32 [32768], P(('panel', 'lag')), may hold values from 0 to 95
- history: bfloat16 [8, 12288, 128], P('lag', 'panel'), may hold values from -6 to 6
- retarded: bfloat16 [8, 96, 16, 128, 128], P('lag', 'panel'), may hold values from -0.046875 to 0.046875
- columns: int32 [8, 96, 16], P('lag', 'panel'), may hold values from 0 to 95, all different within a row
- inverse: float32 [96, 128, 128], P('panel'), may hold values from -0.5 to 0.5
Outputs:
- solutions: bfloat16 [3, 12288, 128], P(None, 'panel')
Inputs may be any that keep to these rules, and one draw needn't show every extreme that they name: `columns`: each row of a lag names 16 different column blocks.
All inputs are finite; a program needn't handle non-finite values.
Results may differ from a plain program's by a relative error of at most 0.0026.
Values may be sent and summed in bfloat16 or wider, within the bound.
A program may use at most 192 MiB of HBM per device.

v0:
```python
import jax
import jax.numpy as jnp
from jax import lax
from jax.sharding import PartitionSpec as P


def passed_along(array, axis, by):
    size = lax.axis_size(axis)
    pairs = [(i, i + by) for i in range(size) if 0 <= i + by < size]
    return lax.ppermute(array, axis, pairs)


def lag_product(matrices, column_ids, field_blocks):
    chosen = field_blocks[column_ids]
    return jnp.einsum("rkbc,rkcn->rbn", matrices, chosen, preferred_element_type=jnp.float32)


def apply_inverse(inverse, values):
    blocks = values.reshape(inverse.shape[0], inverse.shape[1], -1)
    result = jnp.einsum("rbc,rcn->rbn", inverse, blocks, precision=lax.Precision.HIGHEST)
    return result.reshape(inverse.shape[0] * inverse.shape[1], -1)


def local(strengths, incident_green, targets, history, retarded, columns, inverse):
    lag_dev = history.shape[0]
    own_rows = history.shape[1]
    cases = history.shape[2]
    width = inverse.shape[1]
    own_blocks = inverse.shape[0]
    green_count = incident_green.shape[0]
    cell_blocks = strengths.shape[0] // width
    steps = strengths.shape[1] // cases
    all_blocks = own_blocks * lax.axis_size("panel")
    cell_rows = strengths.reshape(cell_blocks, width, steps * cases)
    green = incident_green.reshape(cell_blocks, green_count // cell_blocks, width, width)
    contrib = jnp.einsum("gibc,gcn->gibn", green, cell_rows, preferred_element_type=jnp.float32)
    contrib = contrib.reshape(green_count, width, steps * cases)
    partial_value = jax.ops.segment_sum(contrib, targets, num_segments=all_blocks).reshape(
        all_blocks * width, steps * cases
    )
    incident_part = lax.psum_scatter(partial_value, "panel", scatter_dimension=0, tiled=True)
    younger = passed_along(history, "lag", 1)
    extended = jnp.concatenate([younger, history], 0)
    gathered = lax.all_gather(extended, "panel", axis=1, tiled=True)
    gathered = gathered.reshape(extended.shape[0], all_blocks, width, cases)
    leading = (lax.axis_index("lag") == 0).astype(jnp.float32)
    solved = []
    new_blocks = []
    for moment in range(steps):
        running = jnp.zeros((own_blocks, width, cases), jnp.float32)
        for lag_local in range(lag_dev):
            running = running + lag_product(
                retarded[lag_local], columns[lag_local], gathered[lag_local + steps - 1 - moment]
            )
        for lag_number in range(1, moment + 1):
            running = running + leading * lag_product(
                retarded[lag_number - 1], columns[lag_number - 1], new_blocks[moment - lag_number]
            )
        running = running.reshape(own_rows, cases)
        local_rhs = incident_part[:, moment * cases : (moment + 1) * cases] - running
        rhs_total = lax.psum(local_rhs, "lag")
        solution = apply_inverse(inverse, rhs_total).astype(jnp.bfloat16)
        solved.append(solution)
        if moment + 1 < steps:
            spread_out = lax.all_gather(solution, "panel", axis=0, tiled=True)
            new_blocks.append(spread_out.reshape(all_blocks, width, cases))
    return jnp.stack(solved)


def solution(mesh):
    placed = (
        P(("panel", "lag"), None),
        P(("panel", "lag"), None, None),
        P(("panel", "lag")),
        P("lag", "panel", None),
        P("lag", "panel", None, None, None),
        P("lag", "panel", None),
        P("panel", None, None),
    )
    return jax.shard_map(
        local, mesh=mesh, in_specs=placed, out_specs=P(None, "panel", None), check_vma=False
    )
```

profile of v0, /device:TPU:65, one launch (start us, length us, event | category | flops | bytes accessed | tf_op | source)
XLA Modules:
  0.0 539.5 jit_solution(9330547996670660863)
XLA Ops:
  6.5 3.4 collective-permute-start
  9.9 4.6 collective-permute-done
  14.5 1.7 pad_maximum_fusion
  16.4 22.0 %fusion.84 = f32[8,32,128,384]{3,2,1,0:T(8,128)} fusion(bf16[8,32,128,128]{3,2,1,0:T(8,128)(2,1)} %bitcast.180, bf16[8,128,384,1]{2,1,3,0:T(8,128)(2,1)S(1)} %bitcast.173), kind=kOutput, calls=%fused_computation.70 | convolution fusion | flops 3221225472 | bytes 59506688 | tf_op jit(solution)/shard_map/gibc,gcn->gibn/dot_general | solution.py:36
  38.3 8.7 %broadcast_in_dim.4 = f32[96,128,384]{2,1,0:T(8,128)} broadcast(f32[]{:T(128)} %constant.4.clone.1), dimensions={} | broadcast | bytes 18874372 | tf_op jit(solution)/shard_map/broadcast_in_dim | solution.py:38
  47.0 124.7 %scatter_fusion = f32[96,128,384]{2,1,0:T(8,128)} fusion(f32[96,128,384]{2,1,0:T(8,128)} %broadcast_in_dim.4, s32[256]{0:T(256)S(1)} %copy-done.12, f32[256,128,384]{2,1,0:T(8,128)} %bitcast.175), kind=kCustom, calls=%fused_computation.9 | custom fusion | flops 12582912 | bytes 150995968 | tf_op jit(solution)/shard_map/scatter-add | solution.py:38
  172.7 9.1 %fusion.83 = (bf16[1,12288,128]{2,1,0:T(8,128)(2,1)}, bf16[1,12288,128]{2,1,0:T(8,128)(2,1)}, bf16[1,12288,128]{2,1,0:T(8,128)(2,1)}, bf16[1,12288,128]{2,1,0:T(8,128)(2,1)}) fusion(bf16[4,12288,128]{2,1,0:T(8,128)(2,1)} %all-gather.4.cloned.1.call-done), kind=kLoop, calls=%fused_computation.69 | loop fusion | bytes 25165824 | tf_op jit(solution)/shard_map/slice | solution.py:53
  181.8 4.3 gather_fusion
  186.1 3.1 gather_fusion.1
  189.2 2.9 fusion.30
  193.3 101.5 %reduce-scatter.2.cloned.1.call-done = f32[384,384]{1,0:T(8,128)} async-done(((f32[12288,384]{1,0:T(8,128)}), f32[384,384]{1,0:T(8,128)}) %reduce-scatter.2.cloned.1.call-update) | async-done | bytes 589840 | tf_op jit(solution)/shard_map/reduce_scatter | solution.py:41
  294.8 1.6 slice_subtract_fusion.2
  296.5 40.0 %all-reduce.4.cloned.1.call-done = f32[3,128,128]{2,1,0:T(8,128)} async-done(((f32[3,128,128]{2,1,0:T(8,128)}), f32[3,128,128]{2,1,0:T(8,128)}) %all-reduce.4.cloned.1.call-update) | async-done | bytes 196624 | tf_op jit(solution)/shard_map/psum | solution.py:61
  336.5 1.9 convolution_convert_fusion.2
  338.4 2.7 gather_fusion.3
  341.2 3.8 gather_fusion.2
  345.0 2.4 fusion.27
  347.5 39.6 %all-gather.6.cloned.1.call-done = bf16[12288,128]{1,0:T(8,128)(2,1)} async-done(((bf16[384,128]{1,0:T(8,128)(2,1)}), bf16[12288,128]{1,0:T(8,128)(2,1)}) %all-gather.6.cloned.1.call-update) | async-done | bytes 3145744 | tf_op jit(solution)/shard_map/all_gather | solution.py:65
  387.1 3.8 gather_fusion.4
  390.9 2.6 fusion.66
  395.6 38.0 %all-reduce.6.cloned.1.call-done = f32[3,128,128]{2,1,0:T(8,128)} async-done(((f32[3,128,128]{2,1,0:T(8,128)}), f32[3,128,128]{2,1,0:T(8,128)}) %all-reduce.6.cloned.1.call-update) | async-done | bytes 196624 | tf_op jit(solution)/shard_map/psum | solution.py:61
  433.6 1.9 convolution_convert_fusion.1
  435.7 3.9 gather_fusion.6
  439.6 2.7 gather_fusion.5
  442.3 2.0 fusion.21
  444.3 2.7 gather_fusion.8
  447.0 2.7 fusion.63
  449.7 34.7 %all-gather.8.cloned.1.call-done = bf16[12288,128]{1,0:T(8,128)(2,1)} async-done(((bf16[384,128]{1,0:T(8,128)(2,1)}), bf16[12288,128]{1,0:T(8,128)(2,1)}) %all-gather.8.cloned.1.call-update) | async-done | bytes 3145744 | tf_op jit(solution)/shard_map/all_gather | solution.py:65
  484.4 4.0 gather_fusion.7
  488.4 2.6 fusion.69
  492.6 38.0 %all-reduce.8.cloned.1.call-done = f32[3,128,128]{2,1,0:T(8,128)} async-done(((f32[3,128,128]{2,1,0:T(8,128)}), f32[3,128,128]{2,1,0:T(8,128)}) %all-reduce.8.cloned.1.call-update) | async-done | bytes 196624 | tf_op jit(solution)/shard_map/psum | solution.py:61
  530.6 1.2 convolution_convert_fusion
  (52 shorter events, 6.9 us)
Async XLA Ops:
  6.5 9.8 %copy-start = (bf16[1024,384]{1,0:T(8,128)(2,1)S(1)}, bf16[1024,384]{1,0:T(8,128)(2,1)}, u32[]{:S(2)}) copy-start(bf16[1024,384]{1,0:T(8,128)(2,1)} %param.7) | copy-start | bytes 2359300
  6.5 166.2 %all-gather.4.cloned.1.call-start = ((), (), s32[]{:S(2)}) async-start(), calls=%async_computation.2 | async-start | bytes 12976128 | tf_op jit(solution)/shard_map/all_gather | solution.py:44
  6.5 8.0 %collective-permute-start = (bf16[2,384,128]{2,1,0:T(8,128)(2,1)}, bf16[2,384,128]{2,1,0:T(8,128)(2,1)S(1)}, u32[]{:S(2)}, u32[]{:S(2)}) collective-permute-start(bf16[2,384,128]{2,1,0:T(8,128)(2,1)} %param.10), channel_id=1, source_target_pairs={{0,1},{1,2},{2,3},{4,5},{5,6},{6,7},{8,9},{9,10},{10,11},{12,13},{... | collective-permute-start | bytes 589832 | tf_op jit(solution)/shard_map/ppermute | solution.py:10
  16.3 278.5 %reduce-scatter.2.cloned.1.call-start = ((), (), s32[]{:S(2)}) async-start(), calls=%async_computation.1 | async-start | bytes 19464192 | tf_op jit(solution)/shard_map/reduce_scatter | solution.py:41
  38.3 8.7 %copy-start.12 = (s32[256]{0:T(256)S(1)}, s32[256]{0:T(256)}, u32[]{:S(2)}) copy-start(s32[256]{0:T(256)} %param.9) | copy-start | bytes 3076
  171.8 0.7 copy-start.11
  171.8 164.7 %all-reduce.4.cloned.1.call-start = ((), (), s32[]{:S(2)}) async-start(), calls=%async_computation.3 | async-start | bytes 393216 | tf_op jit(solution)/shard_map/psum | solution.py:61
  189.2 3.5 copy-start.2
  192.7 143.8 %copy-start.6 = (f32[3,128,128]{2,1,0:T(8,128)S(1)}, f32[3,128,128]{2,1,0:T(8,128)}, u32[]{:S(2)}) copy-start(f32[3,128,128]{2,1,0:T(8,128)} %param.13) | copy-start | bytes 589828
  296.4 90.6 %all-gather.6.cloned.1.call-start = ((), (), s32[]{:S(2)}) async-start(), calls=%async_computation.4 | async-start | bytes 3244032 | tf_op jit(solution)/shard_map/all_gather | solution.py:65
  338.4 95.2 %all-reduce.6.cloned.1.call-start = ((), (), s32[]{:S(2)}) async-start(), calls=%async_computation.5 | async-start | bytes 393216 | tf_op jit(solution)/shard_map/psum | solution.py:61
  390.9 2.8 copy-start.3
  393.7 1.1 copy-start.9
  395.5 88.9 %all-gather.8.cloned.1.call-start = ((), (), s32[]{:S(2)}) async-start(), calls=%async_computation.6 | async-start | bytes 3244032 | tf_op jit(solution)/shard_map/all_gather | solution.py:65
  435.5 95.1 %all-reduce.8.cloned.1.call-start = ((), (), s32[]{:S(2)}) async-start(), calls=%async_computation.7 | async-start | bytes 393216 | tf_op jit(solution)/shard_map/psum | solution.py:61
  484.4 6.6 %copy-start.5 = (bf16[48,128,128]{2,1,0:T(8,128)(2,1)S(1)}, bf16[48,128,128]{2,1,0:T(8,128)(2,1)}, u32[]{:S(2)}) copy-start(bf16[48,128,128]{2,1,0:T(8,128)(2,1)} %gather_fusion.6) | copy-start | bytes 4718596
  488.4 2.8 copy-start.4
  488.4 2.8 copy-start.10
  491.2 40.6 %copy-start.7 = (bf16[3,128,128]{1,2,0:T(8,128)(2,1)S(1)}, bf16[3,128,128]{1,2,0:T(8,128)(2,1)}, u32[]{:S(2)}) copy-start(bf16[3,128,128]{1,2,0:T(8,128)(2,1)} %convolution_convert_fusion.2) | copy-start | bytes 294916
  491.2 40.6 %copy-start.8 = (bf16[3,128,128]{1,2,0:T(8,128)(2,1)S(1)}, bf16[3,128,128]{1,2,0:T(8,128)(2,1)}, u32[]{:S(2)}) copy-start(bf16[3,128,128]{1,2,0:T(8,128)(2,1)} %convolution_convert_fusion.1) | copy-start | bytes 294916
  491.2 41.4 %copy-start.1 = (bf16[1024,384]{1,0:T(8,128)(2,1)S(1)}, bf16[1024,384]{1,0:T(8,128)(2,1)}, u32[]{:S(2)}) copy-start(bf16[1024,384]{1,0:T(8,128)(2,1)} %param.7) | copy-start | bytes 2359300
Sparse Core Ops, SparseCore 0:
  16.4 65.7 all-gather.3
  171.9 122.8 reduce-scatter.1
  297.2 39.1 all-reduce.3
  338.6 48.4 all-gather.5
  395.6 37.8 all-reduce.5
  435.9 48.4 all-gather.7
  492.7 37.8 all-reduce.7
where the time goes:
time: 544 us; the launch traced here: 539 us
  waiting for transfers between devices  297 us (55%)
  other arithmetic  130 us (24%)
  local copies, waits for them, and re-layouts  51.2 us (9%)
  matrix products  43.9 us (8%)
  between operations  13.7 us (3%)
    scatter-add x1, other arithmetic, local(): jax.ops.segment_sum(contrib, targets, num_segments=all_blocks)  125 us
    psum x3, waiting for transfers between devices, local(): rhs_total = lax.psum(local_rhs, 'lag')  116 us
    reduce_scatter x1, waiting for transfers between devices, local(): lax.psum_scatter(partial_value, 'panel', scatter_dimension=0, tiled=True)  102 us
    all_gather x2, waiting for transfers between devices, local(): spread_out = lax.all_gather(solution, 'panel', axis=0, tiled=True)  74.3 us
    gather x9, local copies, waits for them, and re-layouts, lag_product(): chosen = field_blocks[column_ids]  31 us
    dot_general x1, matrix products, local(): jnp.einsum('gibc,gcn->gibn', green, cell_rows, preferred_element_type=jnp...  22 us
    dot_general x9, matrix products, lag_product(): jnp.einsum('rkbc,rkcn->rbn', matrices, chosen, preferred_element_type=jnp...  16.9 us
  transfers between devices with their start and end apart: 8, of which 7 were waited for; matrix products, arithmetic and copies ran while one was open for 37% of the time, Pallas kernels for 0%

commit v1 on v0

--- a/solution.py
+++ b/solution.py
@@ -1,7 +1,66 @@
+import functools
+
 import jax
 import jax.numpy as jnp
 from jax import lax
+from jax.experimental import pallas as pl
+from jax.experimental.pallas import tpu as pltpu
 from jax.sharding import PartitionSpec as P
+
+
+def incident_kernel(per_cell, steps, targets, green, cells, out, total, sem):
+    group = pl.program_id(0)
+    width = green.shape[1]
+
+    @pl.when(group == 0)
+    def clear():
+        total[...] = jnp.zeros_like(total)
+
+    def add_block(i, carry):
+        target = targets[group * per_cell + i]
+        product = jnp.dot(green[i], cells[...], preferred_element_type=jnp.float32)
+        for s in range(steps):
+            total[s, target] += product[:, s * width : (s + 1) * width]
+        return carry
+
+    lax.fori_loop(0, per_cell, add_block, 0, unroll=4)
+
+    @pl.when(group == pl.num_programs(0) - 1)
+    def store():
+        copies = [
+            pltpu.make_async_copy(
+                total.at[s], out.at[:, :, pl.ds(s * width, width)], sem.at[s]
+            )
+            for s in range(steps)
+        ]
+        for copy in copies:
+            copy.start()
+        for copy in copies:
+            copy.wait()
+
+
+def incident_partial(strengths, green, targets, all_blocks, steps):
+    count, width, _ = green.shape
+    cell_blocks = strengths.shape[0] // width
+    per_cell = count // cell_blocks
+    return pl.pallas_call(
+        functools.partial(incident_kernel, per_cell, steps),
+        out_shape=jax.ShapeDtypeStruct((all_blocks, width, strengths.shape[1]), jnp.float32),
+        grid_spec=pltpu.PrefetchScalarGridSpec(
+            num_scalar_prefetch=1,
+            grid=(cell_blocks,),
+            in_specs=[
+                pl.BlockSpec((per_cell, width, width), lambda g, t: (g, 0, 0)),
+                pl.BlockSpec((width, strengths.shape[1]), lambda g, t: (g, 0)),
+            ],
+            out_specs=pl.BlockSpec(memory_space=pl.ANY),
+            scratch_shapes=[
+                pltpu.VMEM((steps, all_blocks, width, width), jnp.float32),
+                pltpu.SemaphoreType.DMA((steps,)),
+            ],
+        ),
+        compiler_params=pltpu.CompilerParams(vmem_limit_bytes=40 * 2**20),
+    )(targets, green, strengths)
 
 
 def passed_along(array, axis, by):
@@ -27,17 +86,10 @@
     cases = history.shape[2]
     width = inverse.shape[1]
     own_blocks = inverse.shape[0]
-    green_count = incident_green.shape[0]
-    cell_blocks = strengths.shape[0] // width
     steps = strengths.shape[1] // cases
     all_blocks = own_blocks * lax.axis_size("panel")
-    cell_rows = strengths.reshape(cell_blocks, width, steps * cases)
-    green = incident_green.reshape(cell_blocks, green_count // cell_blocks, width, width)
-    contrib = jnp.einsum("gibc,gcn->gibn", green, cell_rows, preferred_element_type=jnp.float32)
-    contrib = contrib.reshape(green_count, width, steps * cases)
-    partial_value = jax.ops.segment_sum(contrib, targets, num_segments=all_blocks).reshape(
-        all_blocks * width, steps * cases
-    )
+    partial_value = incident_partial(strengths, incident_green, targets, all_blocks, steps)
+    partial_value = partial_value.reshape(all_blocks * width, steps * cases)
     incident_part = lax.psum_scatter(partial_value, "panel", scatter_dimension=0, tiled=True)
     younger = passed_along(history, "lag", 1)
     extended = jnp.concatenate([younger, history], 0)

time: 544 us -> 455 us (0.84)
  other arithmetic: 130 us -> 7.35 us
  waiting for transfers between devices: 297 us -> 333 us
  Pallas kernels: 0 us -> 25.2 us
  matrix products: 43.9 us -> 20.5 us
    scatter-add x1 -> x0, other arithmetic: 125 us -> none  [local(): jax.ops.segment_sum(contrib, targets, num_segments=all_blocks)]
    all_gather x1, waiting for transfers between devices: 0.02 us -> 35.6 us  [local(): gathered = lax.all_gather(extended, 'panel', axis=1, tiled=True)]
    pallas_call x0 -> x1, Pallas kernels: none -> 25.2 us  [incident_partial(): pl.pallas_call(functools.partial(incident_kernel, per_cell, steps), out_s...]
    dot_general x1 -> x0, matrix products: 22 us -> none  [local(): jnp.einsum('gibc,gcn->gibn', green, cell_rows, preferred_element_type=jnp...]
    broadcast_in_dim x1 -> x0, local copies, waits for them, and re-layouts: 8.72 us -> none  [local(): jax.ops.segment_sum(contrib, targets, num_segments=all_blocks)]
  transfers between devices with their start and end apart: 8 -> 8, of which waited for: 7 -> 8; matrix products, arithmetic and copies ran while one was open for 37% -> 10% of each run, Pallas kernels for 0% -> 6%
where the time goes in v1:
time: 455 us; the launch traced here: 450 us
  waiting for transfers between devices  333 us (73%)
  local copies, waits for them, and re-layouts  47 us (10%)
  Pallas kernels  25.2 us (6%)
  matrix products  20.5 us (5%)
  between operations  13.7 us (3%)
  other arithmetic  7.35 us (2%)
    psum x3, waiting for transfers between devices, local(): rhs_total = lax.psum(local_rhs, 'lag')  116 us
    reduce_scatter x1, waiting for transfers between devices, local(): lax.psum_scatter(partial_value, 'panel', scatter_dimension=0, tiled=True)  106 us
    all_gather x2, waiting for transfers between devices, local(): spread_out = lax.all_gather(solution, 'panel', axis=0, tiled=True)  70.8 us
    all_gather x1, waiting for transfers between devices, local(): gathered = lax.all_gather(extended, 'panel', axis=1, tiled=True)  35.6 us
    gather x9, local copies, waits for them, and re-layouts, lag_product(): chosen = field_blocks[column_ids]  33.5 us
    pallas_call x1, Pallas kernels, incident_partial(): pl.pallas_call(functools.partial(incident_kernel, per_cell, steps), out_s...  25.2 us
    dot_general x9, matrix products, lag_product(): jnp.einsum('rkbc,rkcn->rbn', matrices, chosen, preferred_element_type=jnp...  15.5 us
  transfers between devices with their start and end apart: 8, of which 8 were waited for; matrix products, arithmetic and copies ran while one was open for 10% of the time, Pallas kernels for 6%

profile of v1, /device:TPU:65, one launch (start us, length us, event | category | flops | bytes accessed | tf_op | source)
XLA Modules:
  0.0 450.4 jit_solution(6443935528576614120)
XLA Ops:
  6.5 3.4 collective-permute-start
  9.9 4.6 %collective-permute-done = bf16[2,384,128]{2,1,0:T(8,128)(2,1)S(1)} collective-permute-done((bf16[2,384,128]{2,1,0:T(8,128)(2,1)}, bf16[2,384,128]{2,1,0:T(8,128)(2,1)S(1)}, u32[]{:S(2)}, u32[]{:S(2)}) %collective-permute-start) | collective-permute-done | bytes 196640 | tf_op jit(solution)/shard_map/ppermute | solution.py:69
  14.5 1.7 pad_maximum_fusion
  16.3 3.4 copy-done.1
  20.4 25.2 %shard_map.73 = f32[96,128,384]{2,1,0:T(8,128)} custom-call(s32[256]{0:T(256)S(1)} %copy-done.3, bf16[256,128,128]{2,1,0:T(8,128)(2,1)S(1)} %copy-done.1, bf16[1024,384]{1,0:T(8,128)(2,1)S(1)} %copy-done.2), custom_call_target="tpu_custom_call" | custom-call | tf_op jit(solution)/shard_map/pallas_call | solution.py:46
  46.5 35.6 %all-gather.4.cloned.1.call-done = bf16[4,12288,128]{2,1,0:T(8,128)(2,1)} async-done(((bf16[4,384,128]{2,1,0:T(8,128)(2,1)}), bf16[4,12288,128]{2,1,0:T(8,128)(2,1)}) %all-gather.4.cloned.1.call-update) | async-done | bytes 12582928 | tf_op jit(solution)/shard_map/all_gather | solution.py:96
  82.1 8.6 %fusion.83 = (bf16[1,12288,128]{2,1,0:T(8,128)(2,1)}, bf16[1,12288,128]{2,1,0:T(8,128)(2,1)}, bf16[1,12288,128]{2,1,0:T(8,128)(2,1)S(1)}, bf16[1,12288,128]{2,1,0:T(8,128)(2,1)}) fusion(bf16[4,12288,128]{2,1,0:T(8,128)(2,1)} %all-gather.4.cloned.1.call-done), kind=kLoop, calls=%fused_computation.68 | loop fusion | bytes 25165824 | tf_op jit(solution)/shard_map/slice | solution.py:105
  90.7 2.0 gather_fusion.1
  92.7 4.4 gather_fusion
  97.1 2.3 fusion.30
  100.0 105.7 %reduce-scatter.2.cloned.1.call-done = f32[384,384]{1,0:T(8,128)} async-done(((f32[12288,384]{1,0:T(8,128)}), f32[384,384]{1,0:T(8,128)}) %reduce-scatter.2.cloned.1.call-update) | async-done | bytes 589840 | tf_op jit(solution)/shard_map/reduce_scatter | solution.py:93
  207.4 40.0 %all-reduce.4.cloned.1.call-done = f32[3,128,128]{2,1,0:T(8,128)} async-done(((f32[3,128,128]{2,1,0:T(8,128)}), f32[3,128,128]{2,1,0:T(8,128)}) %all-reduce.4.cloned.1.call-update) | async-done | bytes 196624 | tf_op jit(solution)/shard_map/psum | solution.py:113
  247.5 1.9 convolution_convert_fusion.2
  249.4 3.8 gather_fusion.3
  253.3 3.9 gather_fusion.2
  257.2 2.0 fusion.27
  259.1 38.9 %all-gather.6.cloned.1.call-done = bf16[12288,128]{1,0:T(8,128)(2,1)} async-done(((bf16[384,128]{1,0:T(8,128)(2,1)}), bf16[12288,128]{1,0:T(8,128)(2,1)}) %all-gather.6.cloned.1.call-update) | async-done | bytes 3145744 | tf_op jit(solution)/shard_map/all_gather | solution.py:117
  298.1 3.9 gather_fusion.4
  302.0 2.1 fusion.66
  304.7 1.6 slice_subtract_fusion.1
  306.4 38.0 %all-reduce.6.cloned.1.call-done = f32[3,128,128]{2,1,0:T(8,128)} async-done(((f32[3,128,128]{2,1,0:T(8,128)}), f32[3,128,128]{2,1,0:T(8,128)}) %all-reduce.6.cloned.1.call-update) | async-done | bytes 196624 | tf_op jit(solution)/shard_map/psum | solution.py:113
  344.4 1.9 convolution_convert_fusion.1
  346.3 3.8 gather_fusion.6
  350.2 3.9 gather_fusion.5
  354.1 2.6 fusion.21
  356.7 3.9 gather_fusion.8
  360.7 2.6 fusion.63
  363.3 31.9 %all-gather.8.cloned.1.call-done = bf16[12288,128]{1,0:T(8,128)(2,1)} async-done(((bf16[384,128]{1,0:T(8,128)(2,1)}), bf16[12288,128]{1,0:T(8,128)(2,1)}) %all-gather.8.cloned.1.call-update) | async-done | bytes 3145744 | tf_op jit(solution)/shard_map/all_gather | solution.py:117
  395.2 3.9 gather_fusion.7
  399.1 2.1 fusion.69
  401.9 1.6 slice_subtract_fusion
  403.5 38.0 %all-reduce.8.cloned.1.call-done = f32[3,128,128]{2,1,0:T(8,128)} async-done(((f32[3,128,128]{2,1,0:T(8,128)}), f32[3,128,128]{2,1,0:T(8,128)}) %all-reduce.8.cloned.1.call-update) | async-done | bytes 196624 | tf_op jit(solution)/shard_map/psum | solution.py:113
  (50 shorter events, 7.3 us)
Async XLA Ops:
  6.5 240.9 %copy-start = (f32[3,128,128]{2,1,0:T(8,128)S(1)}, f32[3,128,128]{2,1,0:T(8,128)}, u32[]{:S(2)}) copy-start(f32[3,128,128]{2,1,0:T(8,128)} %param.13) | copy-start | bytes 589828
  6.5 9.8 %copy-start.2 = (bf16[1024,384]{1,0:T(8,128)(2,1)S(1)}, bf16[1024,384]{1,0:T(8,128)(2,1)}, u32[]{:S(2)}) copy-start(bf16[1024,384]{1,0:T(8,128)(2,1)} %cells.1) | copy-start | bytes 2359300
  6.5 75.6 %all-gather.4.cloned.1.call-start = ((), (), s32[]{:S(2)}) async-start(), calls=%async_computation.2 | async-start | bytes 12976128 | tf_op jit(solution)/shard_map/all_gather | solution.py:96
  6.5 8.0 %collective-permute-start = (bf16[2,384,128]{2,1,0:T(8,128)(2,1)}, bf16[2,384,128]{2,1,0:T(8,128)(2,1)S(1)}, u32[]{:S(2)}, u32[]{:S(2)}) collective-permute-start(bf16[2,384,128]{2,1,0:T(8,128)(2,1)} %param.10), channel_id=1, source_target_pairs={{0,1},{1,2},{2,3},{4,5},{5,6},{6,7},{8,9},{9,10},{10,11},{12,13},{... | collective-permute-start | bytes 589832 | tf_op jit(solution)/shard_map/ppermute | solution.py:69
  16.3 189.5 %reduce-scatter.2.cloned.1.call-start = ((), (), s32[]{:S(2)}) async-start(), calls=%async_computation.1 | async-start | bytes 19464192 | tf_op jit(solution)/shard_map/reduce_scatter | solution.py:93
  16.3 3.4 copy-start.1
  19.7 0.7 copy-start.3
  45.6 0.7 copy-start.12
  45.7 201.8 %all-reduce.4.cloned.1.call-start = ((), (), s32[]{:S(2)}) async-start(), calls=%async_computation.3 | async-start | bytes 393216 | tf_op jit(solution)/shard_map/psum | solution.py:113
  92.7 4.4 copy-start.4
  97.1 2.3 copy-start.6
  207.4 90.7 %all-gather.6.cloned.1.call-start = ((), (), s32[]{:S(2)}) async-start(), calls=%async_computation.4 | async-start | bytes 3244032 | tf_op jit(solution)/shard_map/all_gather | solution.py:117
  249.4 95.0 %all-reduce.6.cloned.1.call-start = ((), (), s32[]{:S(2)}) async-start(), calls=%async_computation.5 | async-start | bytes 393216 | tf_op jit(solution)/shard_map/psum | solution.py:113
  302.0 2.1 copy-start.5
  306.3 88.9 %all-gather.8.cloned.1.call-start = ((), (), s32[]{:S(2)}) async-start(), calls=%async_computation.6 | async-start | bytes 3244032 | tf_op jit(solution)/shard_map/all_gather | solution.py:117
  346.3 95.3 %all-reduce.8.cloned.1.call-start = ((), (), s32[]{:S(2)}) async-start(), calls=%async_computation.7 | async-start | bytes 393216 | tf_op jit(solution)/shard_map/psum | solution.py:113
  399.1 2.1 copy-start.7
  399.1 2.1 copy-start.10
  399.1 2.1 copy-start.11
  401.2 41.6 %copy-start.8 = (bf16[3,128,128]{1,2,0:T(8,128)(2,1)S(1)}, bf16[3,128,128]{1,2,0:T(8,128)(2,1)}, u32[]{:S(2)}) copy-start(bf16[3,128,128]{1,2,0:T(8,128)(2,1)} %convolution_convert_fusion.2) | copy-start | bytes 294916
  401.2 41.6 %copy-start.9 = (bf16[3,128,128]{1,2,0:T(8,128)(2,1)S(1)}, bf16[3,128,128]{1,2,0:T(8,128)(2,1)}, u32[]{:S(2)}) copy-start(bf16[3,128,128]{1,2,0:T(8,128)(2,1)} %convolution_convert_fusion.1) | copy-start | bytes 294916
Sparse Core Ops, SparseCore 0:
  16.4 65.7 all-gather.3
  86.1 119.5 reduce-scatter.1
  208.2 39.2 all-reduce.3
  249.6 48.4 all-gather.5
  306.4 37.8 all-reduce.5
  346.7 48.4 all-gather.7
  403.6 37.8 all-reduce.7

commit v2 on v1

v2 whole, which is shorter than its diff:
```python
import functools

import jax
import jax.numpy as jnp
from jax import lax
from jax.experimental import pallas as pl
from jax.experimental.pallas import tpu as pltpu
from jax.sharding import PartitionSpec as P

MESH = pl.DeviceIdType.MESH
RING = 4
SUM = jnp.float32


def passed_along(array, axis, by):
    size = lax.axis_size(axis)
    pairs = [(i, i + by) for i in range(size) if 0 <= i + by < size]
    return lax.ppermute(array, axis, pairs)


def incident_kernel(per_cell, steps, targets, green, cells, out, total, sem):
    group = pl.program_id(0)
    width = green.shape[1]
    own_blocks = total.shape[3]
    quarter = width // RING

    @pl.when(group == 0)
    def clear():
        def one(i, carry):
            total[i // (RING * RING), i % (RING * RING)] = jnp.zeros(total.shape[2:], SUM)
            return carry

        lax.fori_loop(0, steps * RING * RING, one, 0)

    def add_block(i, carry):
        target = targets[group * per_cell + i]
        device, block = target // own_blocks, target % own_blocks
        chip, core = device // 2, device % 2
        product = jnp.dot(green[i], cells[...], preferred_element_type=SUM)
        for s in range(steps):
            total[s, chip, core, block] += product[:, s * width : (s + 1) * width]
        return carry

    lax.fori_loop(0, per_cell, add_block, 0, unroll=4)

    @pl.when(group == pl.num_programs(0) - 1)
    def store():
        copies = []
        for s in range(steps):
            for core in range(2):
                for j in range(RING):
                    copies.append(
                        pltpu.make_async_copy(
                            total.at[s, :, core, :, pl.ds(j * quarter, quarter)],
                            out.at[s, core, j],
                            sem.at[s, core, j],
                        )
                    )
        for copy in copies:
            copy.start()
        for copy in copies:
            copy.wait()


def incident_partial(strengths, green, targets, own_blocks, steps):
    count, width, _ = green.shape
    cell_blocks = strengths.shape[0] // width
    per_cell = count // cell_blocks
    chips = RING * RING
    return pl.pallas_call(
        functools.partial(incident_kernel, per_cell, steps),
        out_shape=jax.ShapeDtypeStruct(
            (steps, 2, RING, chips, own_blocks, width // RING, width), SUM
        ),
        grid_spec=pltpu.PrefetchScalarGridSpec(
            num_scalar_prefetch=1,
            grid=(cell_blocks,),
            in_specs=[
                pl.BlockSpec((per_cell, width, width), lambda g, t: (g, 0, 0)),
                pl.BlockSpec((width, strengths.shape[1]), lambda g, t: (g, 0)),
            ],
            out_specs=pl.BlockSpec(memory_space=pl.ANY),
            scratch_shapes=[
                pltpu.VMEM((steps, chips, 2, own_blocks, width, width), SUM),
                pltpu.SemaphoreType.DMA((steps, 2, RING)),
            ],
        ),
        compiler_params=pltpu.CompilerParams(vmem_limit_bytes=40 * 2**20),
    )(targets, green, strengths)


def add_into(target, *others):
    def one(i, carry):
        value = target[i]
        for other in others:
            value = value + other[i]
        target[i] = value
        return carry

    lax.fori_loop(0, target.shape[0], one, 0)


def march_kernel(
    steps,
    part, own, young, retarded, columns, inverse, out,
    gath, ret, quad, peer, zhalf, zfull, xhalf, xfull, yhalf, yfull,
    hsum, hhalf, hfull, base, new, newer, sols,
    send_sems, recv_sems, local_sems,
):
    panel, z = lax.axis_index("panel"), lax.axis_index("lag")
    c, x, y = panel % 2, (panel // 2) % RING, panel // (2 * RING)
    lags, own_blocks, knz, width, _ = ret.shape
    quarter = width // RING

    def hop(v, by):
        return lax.rem(v + (by + RING), RING)

    def at(yy, xx, cc):
        return (yy * RING + xx) * 2 + cc

    to_x = {d: (at(y, hop(x, d), c), z) for d in (1, -1)}
    to_y = {d: (at(hop(y, d), x, c), z) for d in (1, -1)}
    to_z = {d: (panel, hop(z, d)) for d in (1, -1)}
    to_mate = (at(y, x, 1 - c), z)

    used = [0]

    def copy(src, dst, to):
        i = used[0]
        used[0] += 1
        return pltpu.make_async_remote_copy(
            src_ref=src, dst_ref=dst, send_sem=send_sems.at[i], recv_sem=recv_sems.at[i],
            device_id=to, device_id_type=MESH,
        )

    started = []

    def go(*copies):
        for one in copies:
            one.start()
            started.append(one)

    def landed(*copies):
        for one in copies:
            one.wait_recv()

    class Gather:
        def __init__(self, view):
            whole = slice(None)
            self.first, self.pass_on, self.lines, self.line_on, self.mates = [], [], [], [], []
            for half, (near, wide) in enumerate(((to_x, to_y), (to_y, to_x))):

                def chunk(part, by, half=half):
                    return view(half, part, y, hop(x, by)) if half == 0 else view(half, part, hop(y, by), x)

                def line(part, by, half=half):
                    return view(half, part, hop(y, by), whole) if half == 0 else view(half, part, whole, hop(x, by))

                self.first.append([copy(chunk(None, 0), chunk(None, 0), near[d]) for d in (1, -1)])
                self.pass_on.append([
                    copy(chunk(0, -1), chunk(0, -1), near[1]),
                    copy(chunk(1, 1), chunk(1, 1), near[-1]),
                ])
                self.lines.append([copy(line(None, 0), line(None, 0), wide[d]) for d in (1, -1)])
                self.line_on.append([
                    copy(line(0, -1), line(0, -1), wide[1]),
                    copy(line(1, 1), line(1, 1), wide[-1]),
                ])
                self.mates.append([copy(line(None, by), line(None, by), to_mate) for by in (0, -1, 1, 2)])

        def all_copies(self):
            return [k for group in (self.first, self.pass_on, self.lines, self.line_on, self.mates) for h in group for k in h]

        def start(self, go):
            for half in (0, 1):
                go(*self.first[half])

        def pass_chunks(self, go):
            for half in (0, 1):
                for d in (0, 1):
                    landed(self.first[half][d])
                    go(self.pass_on[half][d])

        def send_lines(self, go):
            for half in (0, 1):
                landed(*self.pass_on[half])
                go(*self.lines[half], self.mates[half][0])

        def pass_lines(self, go):
            for half in (0, 1):
                for d in (0, 1):
                    landed(self.lines[half][d])
                    go(self.line_on[half][d], self.mates[half][1 + d])

        def last_lines(self, go):
            for half in (0, 1):
                landed(*self.line_on[half])
                go(self.mates[half][3])

        def finish(self):
            for half in (0, 1):
                landed(*self.mates[half])

    lead = RING - 2

    def past_view(half, part, yy, xx):
        first = lead * (1 - half)
        if part is None:
            return gath.at[pl.ds(first, 2), c, yy, xx]
        return gath.at[first + part, c, yy, xx]

    def new_view(buffer):
        def view(half, part, yy, xx):
            rows = width // 2
            first = half * rows
            if part is not None:
                rows = rows // 2
                first = first + part * rows
            return buffer.at[c, yy, xx, :, pl.ds(first, rows)]

        def lines(half, part, yy, xx):
            return view(half, part, yy, xx)

        return lines

    past = Gather(past_view)
    spread = [Gather(new_view(new)), Gather(new_view(newer))]

    class Ring:
        def __init__(self, me, to, chunk, part, half, full):
            up, down, far = hop(me, 1), hop(me, -1), hop(me, 2)
            self.mine = chunk(me)
            self.adds = [(part(up, 0), half(0)), (part(down, 1), half(1))]
            self.halves = [copy(part(far, 0), half(0), to[1]), copy(part(far, 1), half(1), to[-1])]
            self.fulls = [copy(chunk(up), full(0), to[1]), copy(chunk(down), full(1), to[-1])]
            self.arrived = [full(0), full(1)]

        def one(self):
            go(*self.halves)

        def two(self):
            for d in (0, 1):
                landed(self.halves[d])
                add_into(*self.adds[d])
                go(self.fulls[d])

        def three(self):
            landed(*self.fulls)

    cores = [copy(part.at[s, 1 - c], peer.at[s], to_mate) for s in range(steps)]
    kept = [pltpu.make_async_copy(part.at[s, c], quad.at[s], local_sems.at[s]) for s in range(steps)]
    matrices = pltpu.make_async_copy(retarded, ret, local_sems.at[steps])
    along_z, along_x, along_y = [], [], []
    for s in range(steps):
        along_z.append(Ring(
            z, to_z, lambda d, s=s: quad.at[s, d], lambda d, h, s=s: quad.at[s, d, pl.ds(2 * h, 2)],
            lambda i, s=s: zhalf.at[s, i], lambda i, s=s: zfull.at[s, i],
        ))
        along_x.append(Ring(
            x, to_x, lambda d, s=s: quad.at[s, z, :, d], lambda d, h, s=s: quad.at[s, z, pl.ds(2 * h, 2), d],
            lambda i, s=s: xhalf.at[s, i], lambda i, s=s: xfull.at[s, i],
        ))
        along_y.append(Ring(
            y, to_y, lambda d, s=s: quad.at[s, z, d, x],
            lambda d, h, s=s: quad.at[s, z, d, x, :, pl.ds(quarter // 2 * h, quarter // 2)],
            lambda i, s=s: yhalf.at[s, i], lambda i, s=s: yfull.at[s, i],
        ))
    older = Ring(
        z, to_z, lambda d: hsum.at[:, :, d], lambda d, h: hsum.at[:, :, d, pl.ds(quarter // 2 * h, quarter // 2)],
        lambda i: hhalf.at[i], lambda i: hfull.at[i],
    )

    right_first, right_on = [], []
    for s in range(steps):
        right_first.append([copy(base.at[s, :, z], base.at[s, :, z], to_z[d]) for d in (1, -1)])
        on = []
        for d, h in ((1, 0), (-1, 1)):
            piece = base.at[s, :, hop(z, -d), pl.ds(quarter // 2 * h, quarter // 2)]
            on.append(copy(piece, piece, to_z[d]))
        right_on.append(on)

    told = {s: [copy(sols.at[s], sols.at[s], to_z[d]) for d in (1, -1)] for s in range(1, steps)}
    told_on = {}
    for s in range(1, steps):
        pieces = [sols.at[s, :, pl.ds(h * (width // 2), width // 2)] for h in (0, 1)]
        told_on[s] = [copy(pieces[0], pieces[0], to_z[1]), copy(pieces[1], pieces[1], to_z[-1])]

    def field(buffer, lead_index, col):
        chip = col // (2 * own_blocks)
        where = ((col // own_blocks) % 2, chip // RING, chip % RING, col % own_blocks)
        return buffer[(*lead_index, *where)]

    def older_sums():
        def row(i, carry):
            lag, r = i // own_blocks, i % own_blocks
            total = jnp.zeros((width, steps * width), SUM)
            for k in range(0, knz, 2):
                left = jnp.concatenate([ret[lag, r, k], ret[lag, r, k + 1]], 1)
                fields = []
                for j in (k, k + 1):
                    col = columns[lag, r, j]
                    fields.append(jnp.concatenate([field(gath, (lag + steps - 1 - s,), col) for s in range(steps)], 1))
                total = total + jnp.dot(left, jnp.concatenate(fields, 0), preferred_element_type=SUM)
            for s in range(steps):
                value = total[:, s * width : (s + 1) * width].reshape(RING, quarter, width)
                hsum[s, r] += value
            return carry

        hsum[...] = jnp.zeros_like(hsum)
        lax.fori_loop(0, lags * own_blocks, row, 0)

    def newer_sum(s, r):
        total = jnp.zeros((width, width), SUM)
        for lag, buffer in ((0, new),) if s == 1 else ((0, newer), (1, new)):
            for k in range(0, knz, 2):
                left = jnp.concatenate([ret[lag, r, k], ret[lag, r, k + 1]], 1)
                fields = [field(buffer, (), columns[lag, r, j]) for j in (k, k + 1)]
                total = total + jnp.dot(left, jnp.concatenate(fields, 0), preferred_element_type=SUM)
        return total

    def solve(s):
        def row(r, carry):
            rhs = base[s, r].reshape(width, width)
            if s:
                rhs = rhs - newer_sum(s, r)
            value = jnp.dot(inverse[r], rhs, precision=lax.Precision.HIGHEST, preferred_element_type=SUM)
            sols[s, r] = value.astype(sols.dtype)
            return carry

        lax.fori_loop(0, own_blocks, row, 0)

    def to_base(s):
        landed(*along_y[s].fulls)
        quad_mine = quad[s, z, y, x] + yfull[s, 0] + yfull[s, 1]
        older_mine = hsum[s, :, z] + hfull[0, s] + hfull[1, s]
        base[s, :, z] = quad_mine - older_mine

    barrier = pltpu.get_barrier_semaphore()
    neighbours = [*to_x.values(), *to_y.values(), *to_z.values(), to_mate]
    for to in neighbours:
        pl.semaphore_signal(barrier, inc=1, device_id=to, device_id_type=MESH)
    pl.semaphore_wait(barrier, len(neighbours))

    for k in kept:
        k.start()
    matrices.start()
    go(cores[0])
    gath[pl.ds(lead, 2), c, y, x] = own[...]
    gath[pl.ds(0, 2), c, y, x] = young[...]
    past.start(go)
    go(*cores[1:])

    def over_cores(s):
        kept[s].wait()
        landed(cores[s])
        add_into(quad.at[s, hop(z, 2)], peer.at[s, hop(z, 2)])
        along_z[s].one()
        for by in (1, -1, 0):
            add_into(quad.at[s, hop(z, by)], peer.at[s, hop(z, by)])

    def z_to_x(s):
        along_z[s].three()
        add_into(along_z[s].mine, *along_z[s].arrived)
        along_x[s].one()

    def x_to_y(s):
        along_x[s].three()
        add_into(along_x[s].mine, *along_x[s].arrived)
        along_y[s].one()

    def right_side(s):
        to_base(s)
        go(*right_first[s])

    def right_pass(s):
        for d in (0, 1):
            landed(right_first[s][d])
            go(right_on[s][d])

    def right_done(s):
        landed(*right_on[s])

    def leading(act):
        pl.when(z == 0)(act)

    def only_start(*copies):
        for one in copies:
            one.start()

    over_cores(0)
    past.pass_chunks(go)
    past.send_lines(go)
    along_z[0].two()
    over_cores(1)
    past.pass_lines(go)
    z_to_x(0)
    along_z[1].two()
    over_cores(2)
    along_x[0].two()
    past.last_lines(go)
    x_to_y(0)
    past.finish()
    matrices.wait()
    older_sums()
    older.one()
    along_y[0].two()
    older.two()
    older.three()
    right_side(0)
    right_pass(0)
    right_done(0)
    solve(0)

    def send_first():
        new[c, y, x] = sols[0]
        spread[0].start(only_start)

    leading(send_first)
    z_to_x(1)
    along_z[2].two()
    leading(lambda: spread[0].pass_chunks(only_start))
    along_x[1].two()
    leading(lambda: spread[0].send_lines(only_start))
    x_to_y(1)
    along_y[1].two()
    leading(lambda: spread[0].pass_lines(only_start))
    right_side(1)
    right_pass(1)
    leading(lambda: spread[0].last_lines(only_start))
    right_done(1)

    def second():
        spread[0].finish()
        solve(1)
        newer[c, y, x] = sols[1]
        spread[1].start(only_start)
        only_start(*told[1])

    leading(second)
    z_to_x(2)
    leading(lambda: spread[1].pass_chunks(only_start))
    along_x[2].two()
    leading(lambda: spread[1].send_lines(only_start))
    x_to_y(2)
    along_y[2].two()
    leading(lambda: spread[1].pass_lines(only_start))
    right_side(2)
    right_pass(2)
    leading(lambda: spread[1].last_lines(only_start))
    right_done(2)

    def third():
        spread[1].finish()
        solve(2)
        only_start(*told[2])
        for gather in spread:
            for one in gather.all_copies():
                one.wait_send()
        for s in range(1, steps):
            for one in told[s]:
                one.wait_send()

    leading(third)

    for place, d in ((1, 0), (RING - 1, 1)):

        @pl.when(z == place)
        def pass_on(d=d):
            for s in range(1, steps):
                landed(told[s][d])
                told_on[s][d].start()
            for s in range(1, steps):
                told_on[s][d].wait_send()

    @pl.when(z == 2)
    def take():
        for s in range(1, steps):
            landed(*told_on[s])

    for one in started:
        one.wait_send()
    out[...] = sols[...]


def march(part, own, young, retarded, columns, inverse, steps):
    lags, own_blocks, knz, width, _ = retarded.shape
    quarter = width // RING
    cases = own.shape[-1]
    piece = (own_blocks, quarter, cases)
    halved = (own_blocks, quarter // 2, cases)
    bf16 = own.dtype
    plane = (2, RING, RING, own_blocks, width, cases)
    copies = 200
    return pl.pallas_call(
        functools.partial(march_kernel, steps),
        out_shape=jax.ShapeDtypeStruct((steps, own_blocks, width, cases), bf16),
        in_specs=[
            pl.BlockSpec(memory_space=pl.ANY),
            pl.BlockSpec(memory_space=pltpu.VMEM),
            pl.BlockSpec(memory_space=pltpu.VMEM),
            pl.BlockSpec(memory_space=pl.ANY),
            pl.BlockSpec(memory_space=pltpu.SMEM),
            pl.BlockSpec(memory_space=pltpu.VMEM),
        ],
        out_specs=pl.BlockSpec(memory_space=pltpu.VMEM),
        scratch_shapes=[
            pltpu.VMEM((RING, *plane), bf16),
            pltpu.VMEM(retarded.shape, bf16),
            pltpu.VMEM((steps, RING, RING, RING, *piece), SUM),
            pltpu.VMEM((steps, RING, RING, RING, *piece), SUM),
            pltpu.VMEM((steps, 2, RING // 2, RING, *piece), SUM),
            pltpu.VMEM((steps, 2, RING, RING, *piece), SUM),
            pltpu.VMEM((steps, 2, RING // 2, *piece), SUM),
            pltpu.VMEM((steps, 2, RING, *piece), SUM),
            pltpu.VMEM((steps, 2, *halved), SUM),
            pltpu.VMEM((steps, 2, *piece), SUM),
            pltpu.VMEM((steps, own_blocks, RING, quarter, cases), SUM),
            pltpu.VMEM((2, steps, *halved), SUM),
            pltpu.VMEM((2, steps, *piece), SUM),
            pltpu.VMEM((steps, own_blocks, RING, quarter, cases), SUM),
            pltpu.VMEM(plane, bf16),
            pltpu.VMEM(plane, bf16),
            pltpu.VMEM((steps, own_blocks, width, cases), bf16),
            pltpu.SemaphoreType.DMA((copies,)),
            pltpu.SemaphoreType.DMA((copies,)),
            pltpu.SemaphoreType.DMA((steps + 1,)),
        ],
        compiler_params=pltpu.CompilerParams(
            collective_id=0, has_side_effects=True, vmem_limit_bytes=60 * 2**20
        ),
    )(part, own, young, retarded, columns, inverse)


def local(strengths, incident_green, targets, history, retarded, columns, inverse):
    own_rows = history.shape[1]
    cases = history.shape[2]
    width = inverse.shape[1]
    own_blocks = inverse.shape[0]
    steps = strengths.shape[1] // cases
    younger = passed_along(history, "lag", 1)
    part = incident_partial(strengths, incident_green, targets, own_blocks, steps)
    part = part.reshape(steps, 2, RING, RING, RING, own_blocks, width // RING, cases)
    blocked = (history.shape[0], own_blocks, width, cases)
    solved = march(
        part, history.reshape(blocked), younger.reshape(blocked), retarded, columns, inverse, steps
    )
    return solved.reshape(steps, own_rows, cases)


def solution(mesh):
    placed = (
        P(("panel", "lag"), None),
        P(("panel", "lag"), None, None),
        P(("panel", "lag")),
        P("lag", "panel", None),
        P("lag", "panel", None, None, None),
        P("lag", "panel", None),
        P("panel", None, None),
    )
    return jax.shard_map(
        local, mesh=mesh, in_specs=placed, out_specs=P(None, "panel", None), check_vma=False
    )
```

time: 455 us -> 193 us (0.42)
  waiting for transfers between devices: 333 us -> 0.01 us
  Pallas kernels: 25.2 us -> 177 us
  local copies, waits for them, and re-layouts: 47 us -> 8.84 us
  matrix products: 20.5 us -> 0 us
  between operations: 13.7 us -> 0.04 us
  other arithmetic: 7.35 us -> 0 us
    pallas_call x0 -> x1, Pallas kernels: none -> 152 us  [march(): pl.pallas_call(functools.partial(march_kernel, steps), out_shape=jax.Shap...]
    psum x3 -> x0, waiting for transfers between devices: 116 us -> none  [local(): rhs_total = lax.psum(local_rhs, 'lag')]
    all_gather x3 -> x0, waiting for transfers between devices: 106 us -> none  [the longest x2 70.8 us: local(): spread_out = lax.all_gather(solution, 'panel', axis=0, tiled=True)]
    reduce_scatter x1 -> x0, waiting for transfers between devices: 106 us -> none  [local(): lax.psum_scatter(partial_value, 'panel', scatter_dimension=0, tiled=True)]
    gather x9 -> x0, local copies, waits for them, and re-layouts: 33.5 us -> none  [lag_product(): chosen = field_blocks[column_ids]]
    dot_general x12 -> x0, matrix products: 20.5 us -> none  [the longest x9 15.5 us: lag_product(): jnp.einsum('rkbc,rkcn->rbn', matrices, chosen, preferred_element_type=jnp...]
    slice x1 -> x0, local copies, waits for them, and re-layouts: 8.59 us -> none  [local(): gathered[lag_local + steps - 1 - moment]]
    sub x3 -> x0, other arithmetic: 4.86 us -> none  [local(): local_rhs = incident_part[:, moment * cases:(moment + 1) * cases] - running]
  transfers between devices with their start and end apart: 8 -> 1, of which waited for: 8 -> 0; matrix products, arithmetic and copies ran while one was open for 10% -> 1% of each run, Pallas kernels for 6% -> 13%
where the time goes in v2:
time: 193 us; the launch traced here: 190 us
  Pallas kernels  177 us (92%)
  local copies, waits for them, and re-layouts  8.84 us (5%)
  starting transfers between devices  3.24 us (2%)
    pallas_call x1, Pallas kernels, march(): pl.pallas_call(functools.partial(march_kernel, steps), out_shape=jax.Shap...  152 us
    pallas_call x1, Pallas kernels, incident_partial(): pl.pallas_call(functools.partial(incident_kernel, per_cell, steps), out_s...  25.4 us
    unnamed x10, local copies, waits for them, and re-layouts  8.84 us
  transfers between devices with their start and end apart: 1, of which 0 were waited for; matrix products, arithmetic and copies ran while one was open for 1% of the time, Pallas kernels for 13%

profile of v2, /device:TPU:65, one launch (start us, length us, event | category | flops | bytes accessed | tf_op | source)
XLA Modules:
  0.0 189.6 jit_solution(3403890431587330619)
XLA Ops:
  0.0 3.2 %collective-permute-start = (bf16[2,384,128]{2,1,0:T(8,128)(2,1)}, bf16[2,384,128]{2,1,0:T(8,128)(2,1)S(1)}, u32[]{:S(2)}, u32[]{:S(2)}) collective-permute-start(bf16[2,384,128]{2,1,0:T(8,128)(2,1)} %param.10), channel_id=1, source_target_pairs={{0,1},{1,2},{2,3},{4,5},{5,6},{6,7},{8,9},{9,10},{10,11},{12,13},{... | collective-permute-start | bytes 589832 | tf_op jit(solution)/shard_map/ppermute | solution.py:18
  3.3 1.3 copy.8.columns
  4.5 0.0 copy-start
  4.5 3.4 %copy-done = bf16[256,128,128]{2,1,0:T(8,128)(2,1)S(1)} copy-done((bf16[256,128,128]{2,1,0:T(8,128)(2,1)S(1)}, bf16[256,128,128]{2,1,0:T(8,128)(2,1)}, u32[]{:S(2)}) %copy-start) | copy-done | bytes 8388632
  7.9 0.0 copy-start.1
  7.9 1.1 copy-done.1
  9.0 0.0 copy-start.2
  9.0 0.7 copy-done.2
  9.7 25.4 %shard_map.73 = f32[3,2,4,16,3,32,128]{6,5,4,3,2,1,0:T(8,128)} custom-call(s32[256]{0:T(256)S(1)} %copy-done.2, bf16[256,128,128]{2,1,0:T(8,128)(2,1)S(1)} %copy-done, bf16[1024,384]{1,0:T(8,128)(2,1)S(1)} %copy-done.1), custom_call_target="tpu_custom_call" | custom-call | tf_op jit(solution)/shard_map/pallas_call | solution.py:70
  35.1 0.0 collective-permute-done
  35.1 0.0 copy-start.3
  35.1 0.7 copy-done.3
  35.8 152.0 %shard_map.74 = bf16[3,3,128,128]{3,2,1,0:T(8,128)(2,1)} custom-call(f32[3,2,4,4,4,3,32,128]{7,6,5,4,3,2,1,0:T(8,128)} %bitcast.4, bf16[2,3,128,128]{3,2,1,0:T(8,128)(2,1)} %bitcast.6, bf16[2,3,128,128]{3,2,1,0:T(8,128)(2,1)} %bitcast.7, bf16[2,3,16,128,128]{4,3,2,1,0:T(8,128)(2,1)} %retarded.1, s32[2,3,16]{2,1,0:T(4,128)} %copy.8.columns, ...), custom_call_target="tpu_custom_call" | custom-call | tf_op jit(solution)/shard_map/pallas_call | solution.py:494
  187.9 1.7 copy.10
Async XLA Ops:
  0.0 35.1 %collective-permute-start = (bf16[2,384,128]{2,1,0:T(8,128)(2,1)}, bf16[2,384,128]{2,1,0:T(8,128)(2,1)S(1)}, u32[]{:S(2)}, u32[]{:S(2)}) collective-permute-start(bf16[2,384,128]{2,1,0:T(8,128)(2,1)} %param.10), channel_id=1, source_target_pairs={{0,1},{1,2},{2,3},{4,5},{5,6},{6,7},{8,9},{9,10},{10,11},{12,13},{... | collective-permute-start | bytes 589832 | tf_op jit(solution)/shard_map/ppermute | solution.py:18
  4.5 3.4 %copy-start = (bf16[256,128,128]{2,1,0:T(8,128)(2,1)S(1)}, bf16[256,128,128]{2,1,0:T(8,128)(2,1)}, u32[]{:S(2)}) copy-start(bf16[256,128,128]{2,1,0:T(8,128)(2,1)} %green.1) | copy-start | bytes 25165828
  7.9 1.1 copy-start.1
  9.0 0.7 copy-start.2
  35.1 0.7 copy-start.3

commit v3 on v2

v3 whole, which is shorter than its diff:
```python
import functools

import jax
import jax.numpy as jnp
from jax import lax
from jax.experimental import pallas as pl
from jax.experimental.pallas import tpu as pltpu
from jax.sharding import PartitionSpec as P

MESH = pl.DeviceIdType.MESH
RING = 4
SUM = jnp.float32
CODE = jnp.int16
CODES = 32767.0
TINY = 1e-33


def incident_kernel(per_cell, steps, targets, green, cells, out, total, sem):
    group = pl.program_id(0)
    width = green.shape[1]
    own_blocks = total.shape[3]
    quarter = width // RING

    @pl.when(group == 0)
    def clear():
        def one(i, carry):
            total[i // (RING * RING), i % (RING * RING)] = jnp.zeros(total.shape[2:], SUM)
            return carry

        lax.fori_loop(0, steps * RING * RING, one, 0)

    def add_block(i, carry):
        target = targets[group * per_cell + i]
        device, block = target // own_blocks, target % own_blocks
        chip, core = device // 2, device % 2
        product = jnp.dot(green[i], cells[...], preferred_element_type=SUM)
        for s in range(steps):
            total[s, chip, core, block] += product[:, s * width : (s + 1) * width]
        return carry

    lax.fori_loop(0, per_cell, add_block, 0, unroll=4)

    @pl.when(group == pl.num_programs(0) - 1)
    def store():
        copies = []
        for s in range(steps):
            for core in range(2):
                for j in range(RING):
                    copies.append(
                        pltpu.make_async_copy(
                            total.at[s, :, core, :, pl.ds(j * quarter, quarter)],
                            out.at[s, core, j],
                            sem.at[s, core, j],
                        )
                    )
        for copy in copies:
            copy.start()
        for copy in copies:
            copy.wait()


def incident_partial(strengths, green, targets, own_blocks, steps):
    count, width, _ = green.shape
    cell_blocks = strengths.shape[0] // width
    per_cell = count // cell_blocks
    chips = RING * RING
    return pl.pallas_call(
        functools.partial(incident_kernel, per_cell, steps),
        out_shape=jax.ShapeDtypeStruct(
            (steps, 2, RING, chips, own_blocks, width // RING, width), SUM
        ),
        grid_spec=pltpu.PrefetchScalarGridSpec(
            num_scalar_prefetch=1,
            grid=(cell_blocks,),
            in_specs=[
                pl.BlockSpec((per_cell, width, width), lambda g, t: (g, 0, 0)),
                pl.BlockSpec((width, strengths.shape[1]), lambda g, t: (g, 0)),
            ],
            out_specs=pl.BlockSpec(memory_space=pl.ANY),
            scratch_shapes=[
                pltpu.VMEM((steps, chips, 2, own_blocks, width, width), SUM),
                pltpu.SemaphoreType.DMA((steps, 2, RING)),
            ],
        ),
        compiler_params=pltpu.CompilerParams(vmem_limit_bytes=60 * 2**20),
    )(targets, green, strengths)


def add_into(target, *others):
    def one(i, carry):
        value = target[i]
        for other in others:
            value = value + other[i]
        target[i] = value
        return carry

    lax.fori_loop(0, target.shape[0], one, 0)


def scales_of(value):
    top = jnp.max(jnp.abs(value), axis=-2, keepdims=True)
    tiny = top < TINY
    return jnp.where(tiny, 0.0, CODES / jnp.where(tiny, 1.0, top)), jnp.where(tiny, 0.0, top * (1.0 / CODES))


def encode(source, codes, scales):
    def one(i, carry):
        value = source[i]
        there, back = scales_of(value)
        codes[i] = jnp.round(value * there).astype(jnp.int32).astype(codes.dtype)
        scales[i] = jnp.squeeze(back, -2)
        return carry

    lax.fori_loop(0, source.shape[0], one, 0)


def decode(codes, scales, i):
    return codes[i].astype(jnp.int32).astype(SUM) * jnp.expand_dims(scales[i], -2)


def add_decoded(target, *arrived):
    def one(i, carry):
        value = target[i]
        for codes, scales in arrived:
            value = value + decode(codes, scales, i)
        target[i] = value
        return carry

    lax.fori_loop(0, target.shape[0], one, 0)


def march_kernel(
    steps,
    part, own, retarded, columns, inverse, out,
    gath, gath_young, ret, quad, peer, base, new, newer, sols, hsum, hgot, ygot,
    zhalf, zhalf_scale, zfull, zfull_scale, zhalf_out, zhalf_out_scale, zfull_out, zfull_out_scale,
    xgot, xgot_scale, xout, xout_scale,
    send_sems, recv_sems, local_sems,
):
    panel, z = lax.axis_index("panel"), lax.axis_index("lag")
    c, x, y = panel % 2, (panel // 2) % RING, panel // (2 * RING)
    lags, own_blocks, knz, width, _ = ret.shape
    quarter = width // RING
    others = (1, -1, 2)

    def hop(v, by):
        return lax.rem(v + (by + RING), RING)

    def at(yy, xx, cc):
        return (yy * RING + xx) * 2 + cc

    to_x = {d: (at(y, hop(x, d), c), z) for d in others}
    to_y = {d: (at(hop(y, d), x, c), z) for d in others}
    to_z = {d: (panel, hop(z, d)) for d in others}
    to_mate = (at(y, x, 1 - c), z)

    used = [0]

    def copy(src, dst, to):
        i = used[0]
        used[0] += 1
        return pltpu.make_async_remote_copy(
            src_ref=src, dst_ref=dst, send_sem=send_sems.at[i], recv_sem=recv_sems.at[i],
            device_id=to, device_id_type=MESH,
        )

    started = []

    def go(*copies):
        for one in copies:
            one.start()
            started.append(one)

    def only_start(*copies):
        for one in copies:
            one.start()

    def landed(*copies):
        for one in copies:
            one.wait_recv()

    class Gather:
        def __init__(self, view, go):
            whole = slice(None)
            self.go = go
            self.first, self.pass_on, self.lines, self.line_on, self.mates = [], [], [], [], []
            for half, (near, wide) in enumerate(((to_x, to_y), (to_y, to_x))):

                def chunk(part, by, half=half):
                    return view(half, part, y, hop(x, by)) if half == 0 else view(half, part, hop(y, by), x)

                def line(part, by, half=half):
                    return view(half, part, hop(y, by), whole) if half == 0 else view(half, part, whole, hop(x, by))

                def sent(what, part, by, to):
                    return copy(what(part, by), what(part, by), to)

                self.first.append([sent(chunk, None, 0, near[d]) for d in (1, -1)])
                self.pass_on.append([sent(chunk, 0, -1, near[1]), sent(chunk, 1, 1, near[-1])])
                self.lines.append([sent(line, None, 0, wide[d]) for d in (1, -1)])
                self.line_on.append([sent(line, 0, -1, wide[1]), sent(line, 1, 1, wide[-1])])
                self.mates.append([sent(line, None, by, to_mate) for by in (0, -1, 1, 2)])

        def all_copies(self):
            return [k for group in (self.first, self.pass_on, self.lines, self.line_on, self.mates) for h in group for k in h]

        def start(self):
            for half in (0, 1):
                self.go(*self.first[half])

        def pass_chunks(self):
            for d in (0, 1):
                for half in (0, 1):
                    landed(self.first[half][d])
                    self.go(self.pass_on[half][d])

        def send_lines(self):
            for half in (0, 1):
                landed(*self.pass_on[half])
                self.go(*self.lines[half])
            for half in (0, 1):
                self.go(self.mates[half][0])

        def pass_lines(self):
            for d in (0, 1):
                for half in (0, 1):
                    landed(self.lines[half][d])
                    self.go(self.line_on[half][d])
            for d in (0, 1):
                for half in (0, 1):
                    self.go(self.mates[half][1 + d])

        def last_lines(self):
            for half in (0, 1):
                landed(*self.line_on[half])
                self.go(self.mates[half][3])

        def finish(self):
            for half in (0, 1):
                landed(*self.mates[half])

        def wait_sends(self):
            for one in self.all_copies():
                one.wait_send()

    def halves_of(buffer, *front):
        def view(half, part, yy, xx):
            rows = width // 2
            first = half * rows
            if part is not None:
                rows = rows // 2
                first = first + part * rows
            return buffer.at[(*front, c, yy, xx, slice(None), pl.ds(first, rows))]

        return view

    past = Gather(halves_of(gath, slice(None)), go)
    young = Gather(halves_of(gath_young, slice(None)), only_start)
    spread = [Gather(halves_of(buffer), only_start) for buffer in (new, newer)]
    younger = copy(own, gath_young.at[:, c, y, x], to_z[1])

    cores = [copy(part.at[s, 1 - c], peer.at[s], to_mate) for s in range(steps)]
    kept = [pltpu.make_async_copy(part.at[s, c], quad.at[s], local_sems.at[s]) for s in range(steps)]
    matrices = pltpu.make_async_copy(retarded, ret, local_sems.at[steps])

    def both(codes, scales, got, got_scales, to):
        return [copy(codes, got, to), copy(scales, got_scales, to)]

    z_halves, z_fulls, x_all, y_all = [], [], [], []
    for s in range(steps):
        z_halves.append([
            both(zhalf_out.at[s, i], zhalf_out_scale.at[s, i], zhalf.at[s, i], zhalf_scale.at[s, i], to_z[d])
            for i, d in enumerate((1, -1))
        ])
        z_fulls.append([
            both(zfull_out.at[s, i], zfull_out_scale.at[s, i], zfull.at[s, i], zfull_scale.at[s, i], to_z[d])
            for i, d in enumerate((1, -1))
        ])
        x_all.append([
            both(xout.at[s, i], xout_scale.at[s, i], xgot.at[s, i], xgot_scale.at[s, i], to_x[d])
            for i, d in enumerate(others)
        ])
        y_all.append([copy(quad.at[s, z, hop(y, d), x], ygot.at[s, i], to_y[d]) for i, d in enumerate(others)])

    def over_cores(s):
        kept[s].wait()
        landed(cores[s])
        far = hop(z, 2)
        add_into(quad.at[s, far], peer.at[s, far])
        for i in (0, 1):
            encode(quad.at[s, far, pl.ds(2 * i, 2)], zhalf_out.at[s, i], zhalf_out_scale.at[s, i])
            go(*z_halves[s][i])
        for by in (1, -1, 0):
            add_into(quad.at[s, hop(z, by)], peer.at[s, hop(z, by)])

    def z_pass(s):
        for i, d in enumerate((1, -1)):
            landed(*z_halves[s][i])
            there = hop(z, d)
            add_decoded(quad.at[s, there, pl.ds(2 * i, 2)], (zhalf.at[s, i], zhalf_scale.at[s, i]))
            encode(quad.at[s, there], zfull_out.at[s, i], zfull_out_scale.at[s, i])
            go(*z_fulls[s][i])

    def z_to_x(s):
        for i in (0, 1):
            landed(*z_fulls[s][i])
        add_decoded(quad.at[s, z], *((zfull.at[s, i], zfull_scale.at[s, i]) for i in (0, 1)))
        for i, d in enumerate(others):
            encode(quad.at[s, z, :, hop(x, d)], xout.at[s, i], xout_scale.at[s, i])
            go(*x_all[s][i])

    def x_to_y(s):
        for one in x_all[s]:
            landed(*one)
        add_decoded(quad.at[s, z, :, x], *((xgot.at[s, i], xgot_scale.at[s, i]) for i in range(3)))
        go(*y_all[s])

    groups = ((0, 1), (1, steps - 1))
    older = [
        [
            copy(hsum.at[pl.ds(first, n), :, hop(z, d)], hgot.at[i, pl.ds(first, n)], to_z[d])
            for i, d in enumerate(others)
        ]
        for first, n in groups
    ]
    right = [[copy(base.at[s, :, z], base.at[s, :, z], to_z[d]) for d in others] for s in range(steps)]

    def right_side(s):
        landed(*y_all[s])
        total = quad[s, z, y, x] - hsum[s, :, z]
        for i in range(3):
            total = total + (ygot[s, i] - hgot[i, s])
        base[s, :, z] = total
        go(*right[s])

    told = {s: [copy(sols.at[s], sols.at[s], to_z[d]) for d in (1, -1)] for s in range(1, steps)}
    told_on = {}
    for s in range(1, steps):
        pieces = [sols.at[s, :, pl.ds(h * (width // 2), width // 2)] for h in (0, 1)]
        told_on[s] = [copy(pieces[0], pieces[0], to_z[1]), copy(pieces[1], pieces[1], to_z[-1])]

    def field(buffer, front, col):
        chip = col // (2 * own_blocks)
        where = ((col // own_blocks) % 2, chip // RING, chip % RING, col % own_blocks)
        return buffer[(*front, *where)]

    def pairs(lag, r, fields):
        total = None
        for k in range(0, knz, 2):
            left = jnp.concatenate([ret[lag, r, k], ret[lag, r, k + 1]], 1)
            low = jnp.concatenate([fields(columns[lag, r, k]), fields(columns[lag, r, k + 1])], 0)
            product = jnp.dot(left, low, preferred_element_type=SUM)
            total = product if total is None else total + product
        return total

    def older_sums(first, n):
        def row(r, carry):
            total = None
            for lag in range(lags):

                def fields(col, lag=lag):
                    entries = [lag - s for s in range(first, first + n)]
                    found = [field(gath, (e,), col) if e >= 0 else field(gath_young, (lags + e,), col) for e in entries]
                    return jnp.concatenate(found, 1)

                value = pairs(lag, r, fields)
                total = value if total is None else total + value
            for j in range(n):
                hsum[first + j, r] = total[:, j * width : (j + 1) * width].reshape(RING, quarter, width)
            return carry

        lax.fori_loop(0, own_blocks, row, 0)

    def solve(s):
        def row(r, carry):
            rhs = base[s, r].reshape(width, width)
            if s:
                for lag, buffer in ((0, new),) if s == 1 else ((1, new), (0, newer)):
                    rhs = rhs - pairs(lag, r, lambda col, buffer=buffer: field(buffer, (), col))
            value = jnp.dot(inverse[r], rhs, precision=lax.Precision.HIGHEST, preferred_element_type=SUM)
            sols[s, r] = value.astype(sols.dtype)
            return carry

        lax.fori_loop(0, own_blocks, row, 0)

    def leading(act):
        pl.when(z == 0)(act)

    def following(act):
        pl.when(z > 0)(act)

    barrier = pltpu.get_barrier_semaphore()
    neighbours = [*to_x.values(), *to_y.values(), *to_z.values(), to_mate]
    for to in neighbours:
        pl.semaphore_signal(barrier, inc=1, device_id=to, device_id_type=MESH)
    for k in kept:
        k.start()
    matrices.start()
    gath[:, c, y, x] = own[...]
    pl.semaphore_wait(barrier, len(neighbours))

    go(cores[0])
    past.start()
    pl.when(z < RING - 1)(younger.start)
    go(*cores[1:])

    def nothing_younger():
        def clear(i, carry):
            gath_young[i // (2 * RING), (i // RING) % 2, i % RING] = jnp.zeros(gath_young.shape[3:], gath_young.dtype)
            return carry

        lax.fori_loop(0, 4 * RING, clear, 0)

    leading(nothing_younger)

    def start_young():
        landed(younger)
        young.start()

    over_cores(0)
    past.pass_chunks()
    past.send_lines()
    following(start_young)
    z_pass(0)
    over_cores(1)
    following(young.pass_chunks)
    past.pass_lines()
    following(young.send_lines)
    z_to_x(0)
    z_pass(1)
    over_cores(2)
    past.last_lines()
    x_to_y(0)
    matrices.wait()
    past.finish()
    older_sums(*groups[0])
    go(*older[0])
    z_pass(2)
    landed(*older[0])
    right_side(0)
    following(young.pass_lines)
    landed(*right[0])
    solve(0)

    def send_first():
        new[c, y, x] = sols[0]
        spread[0].start()

    leading(send_first)
    z_to_x(1)
    following(young.last_lines)
    leading(spread[0].pass_chunks)
    x_to_y(1)
    leading(spread[0].send_lines)
    following(young.finish)
    older_sums(*groups[1])
    go(*older[1])
    z_to_x(2)
    leading(spread[0].pass_lines)
    x_to_y(2)
    landed(*older[1])
    right_side(1)
    right_side(2)
    landed(*right[1])

    def second():
        spread[0].last_lines()
        spread[0].finish()
        solve(1)
        newer[c, y, x] = sols[1]
        spread[1].start()
        only_start(*told[1])

    leading(second)
    landed(*right[2])

    def third():
        spread[1].pass_chunks()
        spread[1].send_lines()
        spread[1].pass_lines()
        spread[1].last_lines()
        spread[1].finish()
        solve(2)
        only_start(*told[2])
        for gather in spread:
            gather.wait_sends()
        for s in range(1, steps):
            for one in told[s]:
                one.wait_send()

    leading(third)

    for place, d in ((1, 0), (RING - 1, 1)):

        @pl.when(z == place)
        def pass_on(d=d):
            for s in range(1, steps):
                landed(told[s][d])
                told_on[s][d].start()
            for s in range(1, steps):
                told_on[s][d].wait_send()

    @pl.when(z == 2)
    def take():
        for s in range(1, steps):
            landed(*told_on[s])

    pl.when(z < RING - 1)(younger.wait_send)
    following(young.wait_sends)
    for one in started:
        one.wait_send()
    out[...] = sols[...]


def march(part, own, retarded, columns, inverse, steps):
    lags, own_blocks, knz, width, _ = retarded.shape
    quarter = width // RING
    cases = own.shape[-1]
    piece = (own_blocks, quarter, cases)
    line = (own_blocks, cases)
    bf16 = own.dtype
    plane = (2, RING, RING, own_blocks, width, cases)
    halves, fulls, direct = (steps, 2, RING // 2, RING), (steps, 2, RING, RING), (steps, 3, RING)

    def coded(lead):
        return [pltpu.VMEM((*lead, *piece), CODE), pltpu.VMEM((*lead, *line), SUM)]

    copies = 240
    return pl.pallas_call(
        functools.partial(march_kernel, steps),
        out_shape=jax.ShapeDtypeStruct((steps, own_blocks, width, cases), bf16),
        in_specs=[
            pl.BlockSpec(memory_space=pl.ANY),
            pl.BlockSpec(memory_space=pltpu.VMEM),
            pl.BlockSpec(memory_space=pl.ANY),
            pl.BlockSpec(memory_space=pltpu.SMEM),
            pl.BlockSpec(memory_space=pltpu.VMEM),
        ],
        out_specs=pl.BlockSpec(memory_space=pltpu.VMEM),
        scratch_shapes=[
            pltpu.VMEM((lags, *plane), bf16),
            pltpu.VMEM((lags, *plane), bf16),
            pltpu.VMEM(retarded.shape, bf16),
            pltpu.VMEM((steps, RING, RING, RING, *piece), SUM),
            pltpu.VMEM((steps, RING, RING, RING, *piece), SUM),
            pltpu.VMEM((steps, own_blocks, RING, quarter, cases), SUM),
            pltpu.VMEM(plane, bf16),
            pltpu.VMEM(plane, bf16),
            pltpu.VMEM((steps, own_blocks, width, cases), bf16),
            pltpu.VMEM((steps, own_blocks, RING, quarter, cases), SUM),
            pltpu.VMEM((3, steps, *piece), SUM),
            pltpu.VMEM((steps, 3, *piece), SUM),
            *coded(halves), *coded(fulls), *coded(halves), *coded(fulls),
            *coded(direct), *coded(direct),
            pltpu.SemaphoreType.DMA((copies,)),
            pltpu.SemaphoreType.DMA((copies,)),
            pltpu.SemaphoreType.DMA((steps + 1,)),
        ],
        compiler_params=pltpu.CompilerParams(
            collective_id=0, has_side_effects=True, vmem_limit_bytes=60 * 2**20
        ),
    )(part, own, retarded, columns, inverse)


def local(strengths, incident_green, targets, history, retarded, columns, inverse):
    own_rows = history.shape[1]
    cases = history.shape[2]
    width = inverse.shape[1]
    own_blocks = inverse.shape[0]
    steps = strengths.shape[1] // cases
    part = incident_partial(strengths, incident_green, targets, own_blocks, steps)
    part = part.reshape(steps, 2, RING, RING, RING, own_blocks, width // RING, cases)
    blocked = (history.shape[0], own_blocks, width, cases)
    solved = march(part, history.reshape(blocked), retarded, columns, inverse, steps)
    return solved.reshape(steps, own_rows, cases)


def solution(mesh):
    placed = (
        P(("panel", "lag"), None),
        P(("panel", "lag"), None, None),
        P(("panel", "lag")),
        P("lag", "panel", None),
        P("lag", "panel", None, None, None),
        P("lag", "panel", None),
        P("panel", None, None),
    )
    return jax.shard_map(
        local, mesh=mesh, in_specs=placed, out_specs=P(None, "panel", None), check_vma=False
    )
```

time: 193 us -> 156 us (0.81); the launches traced: 190 us -> 156 us
  Pallas kernels: 177 us -> 153 us
  local copies, waits for them, and re-layouts: 8.84 us -> 2.97 us
  starting transfers between devices: 3.24 us -> 0 us
    pallas_call x1, Pallas kernels: 152 us -> 126 us  [march(): pl.pallas_call(functools.partial(march_kernel, steps), out_shape=jax.Shap...]
    unnamed x10 -> x2, local copies, waits for them, and re-layouts: 8.84 us -> 2.97 us
    ppermute x1 -> x0, starting transfers between devices: 3.24 us -> none  [passed_along(): return lax.ppermute(array, axis, pairs)]
  transfers between devices with their start and end apart: 1 -> 0, of which waited for: 0 -> 0; matrix products, arithmetic and copies ran while one was open for 1% -> 0% of each run, Pallas kernels for 13% -> 0%
where the time goes in v3:
time: 156 us
  Pallas kernels  153 us (98%)
  local copies, waits for them, and re-layouts  2.97 us (2%)
    pallas_call x1, Pallas kernels, march(): pl.pallas_call(functools.partial(march_kernel, steps), out_shape=jax.Shap...  126 us
    pallas_call x1, Pallas kernels, incident_partial(): pl.pallas_call(functools.partial(incident_kernel, per_cell, steps), out_s...  26.8 us

profile of v3, /device:TPU:65, one launch (start us, length us, event | category | flops | bytes accessed | tf_op | source)
XLA Modules:
  0.0 156.3 jit_solution(13439817392533093224)
XLA Ops:
  0.0 1.3 copy.8.columns
  1.3 26.8 %shard_map.73 = f32[3,2,4,16,3,32,128]{6,5,4,3,2,1,0:T(8,128)} custom-call(s32[256]{0:T(256)} %targets.1, bf16[256,128,128]{2,1,0:T(8,128)(2,1)} %green.1, bf16[1024,384]{1,0:T(8,128)(2,1)} %cells.1), custom_call_target="tpu_custom_call" | custom-call | tf_op jit(solution)/shard_map/pallas_call | solution.py:67
  28.1 126.4 %shard_map.74 = bf16[3,3,128,128]{3,2,1,0:T(8,128)(2,1)} custom-call(f32[3,2,4,4,4,3,32,128]{7,6,5,4,3,2,1,0:T(8,128)} %bitcast.3, bf16[2,3,128,128]{3,2,1,0:T(8,128)(2,1)} %bitcast.5, bf16[2,3,16,128,128]{4,3,2,1,0:T(8,128)(2,1)} %retarded.1, s32[2,3,16]{2,1,0:T(4,128)} %copy.8.columns, f32[3,128,128]{2,1,0:T(8,128)} %inverse.1), custom_call_target="tpu_custom_call" | custom-call | tf_op jit(solution)/shard_map/pallas_call | solution.py:529
  154.6 1.7 %copy.10 = bf16[3,384,128]{2,1,0:T(8,128)(2,1)} copy(bf16[3,384,128]{2,1,0:T(8,128)(2,1)} %bitcast.4) | data formatting | bytes 589824

commit v4 on v3

--- a/solution.py
+++ b/solution.py
@@ -169,11 +169,17 @@
     def go(*copies):
         for one in copies:
             one.start()
-            started.append(one)
+            if not any(one is known for known in started):
+                started.append(one)
 
     def only_start(*copies):
         for one in copies:
             one.start()
+
+    def drain(n):
+        for one in started[:n]:
+            one.wait_send()
+        del started[:n]
 
     def landed(*copies):
         for one in copies:
@@ -183,65 +189,83 @@
         def __init__(self, view, go):
             whole = slice(None)
             self.go = go
-            self.first, self.pass_on, self.lines, self.line_on, self.mates = [], [], [], [], []
-            for half, (near, wide) in enumerate(((to_x, to_y), (to_y, to_x))):
-
-                def chunk(part, by, half=half):
-                    return view(half, part, y, hop(x, by)) if half == 0 else view(half, part, hop(y, by), x)
-
-                def line(part, by, half=half):
-                    return view(half, part, hop(y, by), whole) if half == 0 else view(half, part, whole, hop(x, by))
-
-                def sent(what, part, by, to):
-                    return copy(what(part, by), what(part, by), to)
-
-                self.first.append([sent(chunk, None, 0, near[d]) for d in (1, -1)])
-                self.pass_on.append([sent(chunk, 0, -1, near[1]), sent(chunk, 1, 1, near[-1])])
-                self.lines.append([sent(line, None, 0, wide[d]) for d in (1, -1)])
-                self.line_on.append([sent(line, 0, -1, wide[1]), sent(line, 1, 1, wide[-1])])
-                self.mates.append([sent(line, None, by, to_mate) for by in (0, -1, 1, 2)])
-
-        def all_copies(self):
-            return [k for group in (self.first, self.pass_on, self.lines, self.line_on, self.mates) for h in group for k in h]
+            self.first, self.pass_on, self.wide, self.wide_on, self.mates = [], [], [], [], []
+            for half, (near, far) in enumerate(((to_x, to_y), (to_y, to_x))):
+
+                def spot(part, by, wide_by, half=half):
+                    if half == 0:
+                        return view(half, part, hop(y, wide_by), hop(x, by))
+                    return view(half, part, hop(y, by), hop(x, wide_by))
+
+                def line(wide_by, half=half):
+                    return view(half, None, hop(y, wide_by), whole) if half == 0 else view(half, None, whole, hop(x, wide_by))
+
+                def sent(part, by, wide_by, to):
+                    return copy(spot(part, by, wide_by), spot(part, by, wide_by), to)
+
+                self.first.append([sent(None, 0, 0, near[d]) for d in (1, -1)])
+                self.pass_on.append([sent(0, -1, 0, near[1]), sent(1, 1, 0, near[-1])])
+                self.wide.append({by: [sent(None, by, 0, far[d]) for d in (1, -1)] for by in (0, -1, 1, 2)})
+                self.wide_on.append({by: [sent(0, by, -1, far[1]), sent(1, by, 1, far[-1])] for by in (0, -1, 1, 2)})
+                self.mates.append([copy(line(by), line(by), to_mate) for by in (0, -1, 1, 2)])
 
         def start(self):
             for half in (0, 1):
                 self.go(*self.first[half])
+            for half in (0, 1):
+                self.go(*self.wide[half][0])
 
         def pass_chunks(self):
-            for d in (0, 1):
+            for d, by in ((0, -1), (1, 1)):
                 for half in (0, 1):
                     landed(self.first[half][d])
                     self.go(self.pass_on[half][d])
-
-        def send_lines(self):
+            for by in (-1, 1):
+                for half in (0, 1):
+                    self.go(*self.wide[half][by])
+
+        def far_chunk(self):
             for half in (0, 1):
                 landed(*self.pass_on[half])
-                self.go(*self.lines[half])
+                self.go(*self.wide[half][2])
             for half in (0, 1):
                 self.go(self.mates[half][0])
 
-        def pass_lines(self):
-            for d in (0, 1):
-                for half in (0, 1):
-                    landed(self.lines[half][d])
-                    self.go(self.line_on[half][d])
+        def pass_wide(self, *which):
+            for by in which:
+                for d in (0, 1):
+                    for half in (0, 1):
+                        landed(self.wide[half][by][d])
+                        self.go(self.wide_on[half][by][d])
+
+        def pass_own(self):
+            self.pass_wide(0)
+
+        def pass_near(self):
+            self.pass_wide(-1, 1)
+
+        def pass_far(self):
+            self.pass_wide(2)
             for d in (0, 1):
                 for half in (0, 1):
                     self.go(self.mates[half][1 + d])
 
-        def last_lines(self):
-            for half in (0, 1):
-                landed(*self.line_on[half])
-                self.go(self.mates[half][3])
-
         def finish(self):
             for half in (0, 1):
+                for by in (0, -1, 1, 2):
+                    landed(*self.wide_on[half][by])
+                self.go(self.mates[half][3])
+            for half in (0, 1):
                 landed(*self.mates[half])
 
         def wait_sends(self):
-            for one in self.all_copies():
-                one.wait_send()
+            for half in (0, 1):
+                for group in (self.first, self.pass_on, self.mates, self.wide, self.wide_on):
+                    members = group[half]
+                    if isinstance(members, dict):
+                        members = [one for pair in members.values() for one in pair]
+                    for one in members:
+                        one.wait_send()
 
     def halves_of(buffer, *front):
         def view(half, part, yy, xx):
@@ -255,67 +279,115 @@
         return view
 
     past = Gather(halves_of(gath, slice(None)), go)
+    between = used[0]
     young = Gather(halves_of(gath_young, slice(None)), only_start)
-    spread = [Gather(halves_of(buffer), only_start) for buffer in (new, newer)]
+    used[0] = between
+    spread = [Gather(halves_of(new), only_start)]
+    used[0] = 0
+    spread.append(Gather(halves_of(newer), only_start))
+    used[0] = 2 * between
     younger = copy(own, gath_young.at[:, c, y, x], to_z[1])
 
-    cores = [copy(part.at[s, 1 - c], peer.at[s], to_mate) for s in range(steps)]
-    kept = [pltpu.make_async_copy(part.at[s, c], quad.at[s], local_sems.at[s]) for s in range(steps)]
-    matrices = pltpu.make_async_copy(retarded, ret, local_sems.at[steps])
+    place, towards = {"z": z, "y": y, "x": x}, {"z": to_z, "y": to_y, "x": to_x}
+    orders = ["zxy"] * (steps - 1) + ["xyz"]
+    ordered = (2, 1, -1, 0)
+    whole = slice(None)
+
+    def cut(array, *front, **where):
+        return array.at[(*front, *(where.get(axis, whole) for axis in "zyx"))]
+
+    cores, kept = [], []
+    for s, (a, _, _) in enumerate(orders):
+        chunks = [{a: hop(place[a], by)} for by in ordered]
+        cores.append([copy(cut(part, s, 1 - c, **at_chunk), cut(peer, s, **at_chunk), to_mate) for at_chunk in chunks])
+        kept.append([
+            pltpu.make_async_copy(cut(part, s, c, **at_chunk), cut(quad, s, **at_chunk), local_sems.at[s, i])
+            for i, at_chunk in enumerate(chunks)
+        ])
+    matrices = pltpu.make_async_copy(retarded, ret, local_sems.at[steps, 0])
 
     def both(codes, scales, got, got_scales, to):
         return [copy(codes, got, to), copy(scales, got_scales, to)]
 
-    z_halves, z_fulls, x_all, y_all = [], [], [], []
-    for s in range(steps):
-        z_halves.append([
-            both(zhalf_out.at[s, i], zhalf_out_scale.at[s, i], zhalf.at[s, i], zhalf_scale.at[s, i], to_z[d])
+    ring_far, ring_free, ring_tied, second_all, third_all = [], [], [], [], []
+    for s, (first, then, last) in enumerate(orders):
+        to = towards[first]
+        ring_far.append([
+            both(zhalf_out.at[s, i], zhalf_out_scale.at[s, i], zhalf.at[s, i], zhalf_scale.at[s, i], to[d])
             for i, d in enumerate((1, -1))
         ])
-        z_fulls.append([
-            both(zfull_out.at[s, i], zfull_out_scale.at[s, i], zfull.at[s, i], zfull_scale.at[s, i], to_z[d])
-            for i, d in enumerate((1, -1))
-        ])
-        x_all.append([
-            both(xout.at[s, i], xout_scale.at[s, i], xgot.at[s, i], xgot_scale.at[s, i], to_x[d])
+
+        def near_half(i, h, s=s, to=to):
+            rows = pl.ds(2 * h, 2)
+            return both(
+                zfull_out.at[s, i, rows], zfull_out_scale.at[s, i, rows], zfull.at[s, i, rows],
+                zfull_scale.at[s, i, rows], to[(1, -1)[i]],
+            )
+
+        ring_free.append([near_half(i, 1 - i) for i in (0, 1)])
+        ring_tied.append([near_half(i, i) for i in (0, 1)])
+        second_all.append([
+            both(xout.at[s, i], xout_scale.at[s, i], xgot.at[s, i], xgot_scale.at[s, i], towards[then][d])
             for i, d in enumerate(others)
         ])
-        y_all.append([copy(quad.at[s, z, hop(y, d), x], ygot.at[s, i], to_y[d]) for i, d in enumerate(others)])
+        third_all.append([
+            copy(
+                cut(quad, s, **{first: place[first], then: place[then], last: hop(place[last], d)}),
+                ygot.at[s, i], towards[last][d],
+            )
+            for i, d in enumerate(others)
+        ])
+
+    def ring_part(s, by, h=None):
+        first, _, last = orders[s]
+        where = {first: hop(place[first], by)}
+        if h is not None:
+            where[last] = pl.ds(2 * h, 2)
+        return cut(quad, s, **where)
+
+    def send_near(s, i, h, copies):
+        rows = pl.ds(2 * h, 2)
+        encode(ring_part(s, (1, -1)[i], h), zfull_out.at[s, i, rows], zfull_out_scale.at[s, i, rows])
+        go(*copies)
 
     def over_cores(s):
-        kept[s].wait()
-        landed(cores[s])
-        far = hop(z, 2)
-        add_into(quad.at[s, far], peer.at[s, far])
+        first = orders[s][0]
+        for j, by in enumerate(ordered):
+            kept[s][j].wait()
+            landed(cores[s][j])
+            add_into(ring_part(s, by), cut(peer, s, **{first: hop(place[first], by)}))
+            if by == 2:
+                for i in (0, 1):
+                    encode(ring_part(s, by, i), zhalf_out.at[s, i], zhalf_out_scale.at[s, i])
+                    go(*ring_far[s][i])
+            elif by:
+                i = (1, -1).index(by)
+                send_near(s, i, 1 - i, ring_free[s][i])
+
+    def ring_pass(s):
+        for i, d in enumerate((1, -1)):
+            landed(*ring_far[s][i])
+            add_decoded(ring_part(s, d, i), (zhalf.at[s, i], zhalf_scale.at[s, i]))
+            send_near(s, i, i, ring_tied[s][i])
+
+    def to_second(s):
+        first, then, _ = orders[s]
         for i in (0, 1):
-            encode(quad.at[s, far, pl.ds(2 * i, 2)], zhalf_out.at[s, i], zhalf_out_scale.at[s, i])
-            go(*z_halves[s][i])
-        for by in (1, -1, 0):
-            add_into(quad.at[s, hop(z, by)], peer.at[s, hop(z, by)])
-
-    def z_pass(s):
-        for i, d in enumerate((1, -1)):
-            landed(*z_halves[s][i])
-            there = hop(z, d)
-            add_decoded(quad.at[s, there, pl.ds(2 * i, 2)], (zhalf.at[s, i], zhalf_scale.at[s, i]))
-            encode(quad.at[s, there], zfull_out.at[s, i], zfull_out_scale.at[s, i])
-            go(*z_fulls[s][i])
-
-    def z_to_x(s):
-        for i in (0, 1):
-            landed(*z_fulls[s][i])
-        add_decoded(quad.at[s, z], *((zfull.at[s, i], zfull_scale.at[s, i]) for i in (0, 1)))
+            landed(*ring_free[s][i], *ring_tied[s][i])
+        add_decoded(ring_part(s, 0), *((zfull.at[s, i], zfull_scale.at[s, i]) for i in (0, 1)))
         for i, d in enumerate(others):
-            encode(quad.at[s, z, :, hop(x, d)], xout.at[s, i], xout_scale.at[s, i])
-            go(*x_all[s][i])
-
-    def x_to_y(s):
-        for one in x_all[s]:
+            encode(cut(quad, s, **{first: place[first], then: hop(place[then], d)}), xout.at[s, i], xout_scale.at[s, i])
+            go(*second_all[s][i])
+
+    def to_third(s):
+        first, then, _ = orders[s]
+        for one in second_all[s]:
             landed(*one)
-        add_decoded(quad.at[s, z, :, x], *((xgot.at[s, i], xgot_scale.at[s, i]) for i in range(3)))
-        go(*y_all[s])
-
-    groups = ((0, 1), (1, steps - 1))
+        mine = cut(quad, s, **{first: place[first], then: place[then]})
+        add_decoded(mine, *((xgot.at[s, i], xgot_scale.at[s, i]) for i in range(3)))
+        go(*third_all[s])
+
+    groups = [(s, 1) for s in range(steps)]
     older = [
         [
             copy(hsum.at[pl.ds(first, n), :, hop(z, d)], hgot.at[i, pl.ds(first, n)], to_z[d])
@@ -326,18 +398,14 @@
     right = [[copy(base.at[s, :, z], base.at[s, :, z], to_z[d]) for d in others] for s in range(steps)]
 
     def right_side(s):
-        landed(*y_all[s])
+        landed(*third_all[s])
         total = quad[s, z, y, x] - hsum[s, :, z]
         for i in range(3):
             total = total + (ygot[s, i] - hgot[i, s])
         base[s, :, z] = total
         go(*right[s])
 
-    told = {s: [copy(sols.at[s], sols.at[s], to_z[d]) for d in (1, -1)] for s in range(1, steps)}
-    told_on = {}
-    for s in range(1, steps):
-        pieces = [sols.at[s, :, pl.ds(h * (width // 2), width // 2)] for h in (0, 1)]
-        told_on[s] = [copy(pieces[0], pieces[0], to_z[1]), copy(pieces[1], pieces[1], to_z[-1])]
+    told = {s: [copy(sols.at[s], sols.at[s], to_z[d]) for d in others] for s in range(1, steps)}
 
     def field(buffer, front, col):
         chip = col // (2 * own_blocks)
@@ -393,16 +461,18 @@
     neighbours = [*to_x.values(), *to_y.values(), *to_z.values(), to_mate]
     for to in neighbours:
         pl.semaphore_signal(barrier, inc=1, device_id=to, device_id_type=MESH)
-    for k in kept:
-        k.start()
+    for pieces in kept:
+        for k in pieces:
+            k.start()
     matrices.start()
     gath[:, c, y, x] = own[...]
     pl.semaphore_wait(barrier, len(neighbours))
 
-    go(cores[0])
+    go(*cores[0])
     past.start()
     pl.when(z < RING - 1)(younger.start)
-    go(*cores[1:])
+    for pieces in cores[1:]:
+        go(*pieces)
 
     def nothing_younger():
         def clear(i, carry):
@@ -419,26 +489,29 @@
 
     over_cores(0)
     past.pass_chunks()
-    past.send_lines()
+    past.far_chunk()
+    ring_pass(0)
+    past.pass_own()
+    over_cores(1)
+    past.pass_near()
+    past.pass_far()
     following(start_young)
-    z_pass(0)
-    over_cores(1)
-    following(young.pass_chunks)
-    past.pass_lines()
-    following(young.send_lines)
-    z_to_x(0)
-    z_pass(1)
-    over_cores(2)
-    past.last_lines()
-    x_to_y(0)
+    to_second(0)
     matrices.wait()
     past.finish()
+    leading(lambda: over_cores(2))
     older_sums(*groups[0])
     go(*older[0])
-    z_pass(2)
+    following(young.pass_chunks)
+    to_third(0)
+    following(young.far_chunk)
     landed(*older[0])
     right_side(0)
-    following(young.pass_lines)
+    ring_pass(1)
+    following(young.pass_own)
+    following(young.pass_near)
+    leading(lambda: ring_pass(2))
+    following(young.pass_far)
     landed(*right[0])
     solve(0)
 
@@ -447,24 +520,28 @@
         spread[0].start()
 
     leading(send_first)
-    z_to_x(1)
-    following(young.last_lines)
-    leading(spread[0].pass_chunks)
-    x_to_y(1)
-    leading(spread[0].send_lines)
+    following(lambda: over_cores(2))
+    to_second(1)
     following(young.finish)
     older_sums(*groups[1])
     go(*older[1])
-    z_to_x(2)
-    leading(spread[0].pass_lines)
-    x_to_y(2)
+    leading(spread[0].pass_chunks)
+    following(lambda: ring_pass(2))
+    leading(spread[0].far_chunk)
+    to_third(1)
     landed(*older[1])
+    leading(spread[0].pass_own)
+    leading(spread[0].pass_near)
+    old = len(started)
     right_side(1)
-    right_side(2)
+    older_sums(*groups[2])
+    go(*older[2])
+    leading(spread[0].pass_far)
+    to_second(2)
+    drain(old)
     landed(*right[1])
 
     def second():
-        spread[0].last_lines()
         spread[0].finish()
         solve(1)
         newer[c, y, x] = sols[1]
@@ -472,44 +549,41 @@
         only_start(*told[1])
 
     leading(second)
+    to_third(2)
+    leading(spread[1].pass_chunks)
+    landed(*older[2])
+    leading(spread[1].far_chunk)
+    right_side(2)
+    leading(spread[0].wait_sends)
+    leading(spread[1].pass_own)
+    leading(spread[1].pass_near)
+    leading(spread[1].pass_far)
     landed(*right[2])
 
     def third():
-        spread[1].pass_chunks()
-        spread[1].send_lines()
-        spread[1].pass_lines()
-        spread[1].last_lines()
         spread[1].finish()
         solve(2)
         only_start(*told[2])
-        for gather in spread:
-            gather.wait_sends()
+        spread[1].wait_sends()
         for s in range(1, steps):
             for one in told[s]:
                 one.wait_send()
 
     leading(third)
 
-    for place, d in ((1, 0), (RING - 1, 1)):
-
-        @pl.when(z == place)
-        def pass_on(d=d):
+    for i, d in enumerate(others):
+
+        @pl.when(z == d % RING)
+        def take(i=i):
             for s in range(1, steps):
-                landed(told[s][d])
-                told_on[s][d].start()
-            for s in range(1, steps):
-                told_on[s][d].wait_send()
-
-    @pl.when(z == 2)
-    def take():
-        for s in range(1, steps):
-            landed(*told_on[s])
+                landed(told[s][i])
 
     pl.when(z < RING - 1)(younger.wait_send)
     following(young.wait_sends)
     for one in started:
         one.wait_send()
     out[...] = sols[...]
+    assert used[0] <= send_sems.shape[0], used[0]
 
 
 def march(part, own, retarded, columns, inverse, steps):
@@ -525,7 +599,7 @@
     def coded(lead):
         return [pltpu.VMEM((*lead, *piece), CODE), pltpu.VMEM((*lead, *line), SUM)]
 
-    copies = 240
+    copies = 196
     return pl.pallas_call(
         functools.partial(march_kernel, steps),
         out_shape=jax.ShapeDtypeStruct((steps, own_blocks, width, cases), bf16),
@@ -554,7 +628,7 @@
             *coded(direct), *coded(direct),
             pltpu.SemaphoreType.DMA((copies,)),
             pltpu.SemaphoreType.DMA((copies,)),
-            pltpu.SemaphoreType.DMA((steps + 1,)),
+            pltpu.SemaphoreType.DMA((steps + 1, RING)),
         ],
         compiler_params=pltpu.CompilerParams(
             collective_id=0, has_side_effects=True, vmem_limit_bytes=60 * 2**20

time: 156 us -> 135 us (0.87)
  Pallas kernels: 153 us -> 131 us
    pallas_call x1, Pallas kernels: 126 us -> 104 us  [march(): pl.pallas_call(functools.partial(march_kernel, steps), out_shape=jax.Shap...]
where the time goes in v4:
time: 135 us; the launch traced here: 134 us
  Pallas kernels  131 us (97%)
  local copies, waits for them, and re-layouts  2.97 us (2%)
    pallas_call x1, Pallas kernels, march(): pl.pallas_call(functools.partial(march_kernel, steps), out_shape=jax.Shap...  104 us
    pallas_call x1, Pallas kernels, incident_partial(): pl.pallas_call(functools.partial(incident_kernel, per_cell, steps), out_s...  26.8 us
    unnamed x2, local copies, waits for them, and re-layouts  2.97 us

profile of v4, /device:TPU:65, one launch (start us, length us, event | category | flops | bytes accessed | tf_op | source)
XLA Modules:
  0.0 134.2 jit_solution(16788221237573033633)
XLA Ops:
  0.0 1.3 copy.8.columns
  1.3 26.8 %shard_map.73 = f32[3,2,4,16,3,32,128]{6,5,4,3,2,1,0:T(8,128)} custom-call(s32[256]{0:T(256)} %targets.1, bf16[256,128,128]{2,1,0:T(8,128)(2,1)} %green.1, bf16[1024,384]{1,0:T(8,128)(2,1)} %cells.1), custom_call_target="tpu_custom_call" | custom-call | tf_op jit(solution)/shard_map/pallas_call | solution.py:67
  28.1 104.3 %shard_map.74 = bf16[3,3,128,128]{3,2,1,0:T(8,128)(2,1)} custom-call(f32[3,2,4,4,4,3,32,128]{7,6,5,4,3,2,1,0:T(8,128)} %bitcast.3, bf16[2,3,128,128]{3,2,1,0:T(8,128)(2,1)} %bitcast.5, bf16[2,3,16,128,128]{4,3,2,1,0:T(8,128)(2,1)} %retarded.1, s32[2,3,16]{2,1,0:T(4,128)} %copy.8.columns, f32[3,128,128]{2,1,0:T(8,128)} %inverse.1), custom_call_target="tpu_custom_call" | custom-call | tf_op jit(solution)/shard_map/pallas_call | solution.py:603
  132.5 1.7 %copy.10 = bf16[3,384,128]{2,1,0:T(8,128)(2,1)} copy(bf16[3,384,128]{2,1,0:T(8,128)(2,1)} %bitcast.4) | data formatting | bytes 589824

commit v5 on v4

--- a/solution.py
+++ b/solution.py
@@ -38,7 +38,7 @@
             total[s, chip, core, block] += product[:, s * width : (s + 1) * width]
         return carry
 
-    lax.fori_loop(0, per_cell, add_block, 0, unroll=4)
+    lax.fori_loop(0, per_cell, add_block, 0, unroll=per_cell)
 
     @pl.when(group == pl.num_programs(0) - 1)
     def store():
@@ -132,7 +132,7 @@
 def march_kernel(
     steps,
     part, own, retarded, columns, inverse, out,
-    gath, gath_young, ret, quad, peer, base, new, newer, sols, hsum, hgot, ygot,
+    gath, gath_young, ret, quad, peer, base, new, newer, sols, aside, hsum, hgot, ygot,
     zhalf, zhalf_scale, zfull, zfull_scale, zhalf_out, zhalf_out_scale, zfull_out, zfull_out_scale,
     xgot, xgot_scale, xout, xout_scale,
     send_sems, recv_sems, local_sems,
@@ -289,7 +289,7 @@
     younger = copy(own, gath_young.at[:, c, y, x], to_z[1])
 
     place, towards = {"z": z, "y": y, "x": x}, {"z": to_z, "y": to_y, "x": to_x}
-    orders = ["zxy"] * (steps - 1) + ["xyz"]
+    orders = ["zxy"] * (steps - 1) + ["yxz"]
     ordered = (2, 1, -1, 0)
     whole = slice(None)
 
@@ -350,9 +350,10 @@
         encode(ring_part(s, (1, -1)[i], h), zfull_out.at[s, i, rows], zfull_out_scale.at[s, i, rows])
         go(*copies)
 
-    def over_cores(s):
+    def over_cores(s, which=ordered):
         first = orders[s][0]
-        for j, by in enumerate(ordered):
+        for by in which:
+            j = ordered.index(by)
             kept[s][j].wait()
             landed(cores[s][j])
             add_into(ring_part(s, by), cut(peer, s, **{first: hop(place[first], by)}))
@@ -405,7 +406,7 @@
         base[s, :, z] = total
         go(*right[s])
 
-    told = {s: [copy(sols.at[s], sols.at[s], to_z[d]) for d in others] for s in range(1, steps)}
+    told = {s: [[copy(sols.at[s, r], sols.at[s, r], to_z[d]) for r in range(own_blocks)] for d in others] for s in range(1, steps)}
 
     def field(buffer, front, col):
         chip = col // (2 * own_blocks)
@@ -416,7 +417,7 @@
         total = None
         for k in range(0, knz, 2):
             left = jnp.concatenate([ret[lag, r, k], ret[lag, r, k + 1]], 1)
-            low = jnp.concatenate([fields(columns[lag, r, k]), fields(columns[lag, r, k + 1])], 0)
+            low = jnp.concatenate([fields(columns[r, lag, k]), fields(columns[r, lag, k + 1])], 0)
             product = jnp.dot(left, low, preferred_element_type=SUM)
             total = product if total is None else total + product
         return total
@@ -439,14 +440,25 @@
 
         lax.fori_loop(0, own_blocks, row, 0)
 
-    def solve(s):
+    def set_aside(lag, buffer):
         def row(r, carry):
-            rhs = base[s, r].reshape(width, width)
-            if s:
-                for lag, buffer in ((0, new),) if s == 1 else ((1, new), (0, newer)):
-                    rhs = rhs - pairs(lag, r, lambda col, buffer=buffer: field(buffer, (), col))
-            value = jnp.dot(inverse[r], rhs, precision=lax.Precision.HIGHEST, preferred_element_type=SUM)
-            sols[s, r] = value.astype(sols.dtype)
+            aside[r] = pairs(lag, r, lambda col: field(buffer, (), col))
+            return carry
+
+        lax.fori_loop(0, own_blocks, row, 0)
+
+    def solve_row(s, r, buffer=None):
+        rhs = base[s, r].reshape(width, width)
+        if s == steps - 1:
+            rhs = rhs - aside[r]
+        if buffer is not None:
+            rhs = rhs - pairs(0, r, lambda col: field(buffer, (), col))
+        value = jnp.dot(inverse[r], rhs, precision=lax.Precision.HIGHEST, preferred_element_type=SUM)
+        sols[s, r] = value.astype(sols.dtype)
+
+    def solve(s, buffer=None):
+        def row(r, carry):
+            solve_row(s, r, buffer)
             return carry
 
         lax.fori_loop(0, own_blocks, row, 0)
@@ -499,19 +511,21 @@
     to_second(0)
     matrices.wait()
     past.finish()
-    leading(lambda: over_cores(2))
+    leading(lambda: over_cores(2, ordered[:1]))
     older_sums(*groups[0])
     go(*older[0])
     following(young.pass_chunks)
     to_third(0)
+    leading(lambda: over_cores(2, ordered[1:]))
     following(young.far_chunk)
     landed(*older[0])
+    ring_pass(1)
     right_side(0)
-    ring_pass(1)
     following(young.pass_own)
     following(young.pass_near)
     leading(lambda: ring_pass(2))
     following(young.pass_far)
+    to_second(1)
     landed(*right[0])
     solve(0)
 
@@ -521,53 +535,57 @@
 
     leading(send_first)
     following(lambda: over_cores(2))
-    to_second(1)
     following(young.finish)
     older_sums(*groups[1])
     go(*older[1])
     leading(spread[0].pass_chunks)
-    following(lambda: ring_pass(2))
+    to_third(1)
     leading(spread[0].far_chunk)
-    to_third(1)
     landed(*older[1])
     leading(spread[0].pass_own)
     leading(spread[0].pass_near)
     old = len(started)
     right_side(1)
+    following(lambda: ring_pass(2))
+    leading(spread[0].pass_far)
+    leading(lambda: to_second(2))
     older_sums(*groups[2])
-    go(*older[2])
-    leading(spread[0].pass_far)
-    to_second(2)
     drain(old)
     landed(*right[1])
 
     def second():
         spread[0].finish()
-        solve(1)
+        solve(1, new)
         newer[c, y, x] = sols[1]
         spread[1].start()
-        only_start(*told[1])
+        for pieces in told[1]:
+            only_start(*pieces)
 
     leading(second)
+    go(*older[2])
+    following(lambda: to_second(2))
+    leading(lambda: set_aside(1, new))
     to_third(2)
     leading(spread[1].pass_chunks)
+    leading(spread[1].far_chunk)
     landed(*older[2])
-    leading(spread[1].far_chunk)
-    right_side(2)
     leading(spread[0].wait_sends)
     leading(spread[1].pass_own)
     leading(spread[1].pass_near)
+    right_side(2)
     leading(spread[1].pass_far)
     landed(*right[2])
 
     def third():
         spread[1].finish()
-        solve(2)
-        only_start(*told[2])
+        for r in range(own_blocks):
+            solve_row(2, r, newer)
+            only_start(*(pieces[r] for pieces in told[2]))
         spread[1].wait_sends()
         for s in range(1, steps):
-            for one in told[s]:
-                one.wait_send()
+            for pieces in told[s]:
+                for one in pieces:
+                    one.wait_send()
 
     leading(third)
 
@@ -576,7 +594,7 @@
         @pl.when(z == d % RING)
         def take(i=i):
             for s in range(1, steps):
-                landed(told[s][i])
+                landed(*told[s][i])
 
     pl.when(z < RING - 1)(younger.wait_send)
     following(young.wait_sends)
@@ -599,7 +617,7 @@
     def coded(lead):
         return [pltpu.VMEM((*lead, *piece), CODE), pltpu.VMEM((*lead, *line), SUM)]
 
-    copies = 196
+    copies = 208
     return pl.pallas_call(
         functools.partial(march_kernel, steps),
         out_shape=jax.ShapeDtypeStruct((steps, own_blocks, width, cases), bf16),
@@ -621,6 +639,7 @@
             pltpu.VMEM(plane, bf16),
             pltpu.VMEM(plane, bf16),
             pltpu.VMEM((steps, own_blocks, width, cases), bf16),
+            pltpu.VMEM((own_blocks, width, cases), SUM),
             pltpu.VMEM((steps, own_blocks, RING, quarter, cases), SUM),
             pltpu.VMEM((3, steps, *piece), SUM),
             pltpu.VMEM((steps, 3, *piece), SUM),
@@ -645,7 +664,7 @@
     part = incident_partial(strengths, incident_green, targets, own_blocks, steps)
     part = part.reshape(steps, 2, RING, RING, RING, own_blocks, width // RING, cases)
     blocked = (history.shape[0], own_blocks, width, cases)
-    solved = march(part, history.reshape(blocked), retarded, columns, inverse, steps)
+    solved = march(part, history.reshape(blocked), retarded, columns.transpose(1, 0, 2), inverse, steps)
     return solved.reshape(steps, own_rows, cases)
 
 

time: 135 us -> 117 us (0.87)
  Pallas kernels: 131 us -> 114 us
    pallas_call x1, Pallas kernels: 104 us -> 95.3 us  [march(): pl.pallas_call(functools.partial(march_kernel, steps), out_shape=jax.Shap...]
    pallas_call x1, Pallas kernels: 26.8 us -> 19 us  [incident_partial(): pl.pallas_call(functools.partial(incident_kernel, per_cell, steps), out_s...]
    unnamed x2 -> x1, local copies, waits for them, and re-layouts: 2.97 us -> 1.69 us
where the time goes in v5:
time: 117 us; the launch traced here: 116 us
  Pallas kernels  114 us (97%)
  local copies, waits for them, and re-layouts  1.69 us (1%)
    pallas_call x1, Pallas kernels, march(): pl.pallas_call(functools.partial(march_kernel, steps), out_shape=jax.Shap...  95.3 us
    pallas_call x1, Pallas kernels, incident_partial(): pl.pallas_call(functools.partial(incident_kernel, per_cell, steps), out_s...  19 us

profile of v5, /device:TPU:65, one launch (start us, length us, event | category | flops | bytes accessed | tf_op | source)
XLA Modules:
  0.0 116.0 jit_solution(15896330906756984691)
XLA Ops:
  0.0 19.0 %shard_map.73 = f32[3,2,4,16,3,32,128]{6,5,4,3,2,1,0:T(8,128)} custom-call(s32[256]{0:T(256)} %targets.1, bf16[256,128,128]{2,1,0:T(8,128)(2,1)} %green.1, bf16[1024,384]{1,0:T(8,128)(2,1)} %cells.1), custom_call_target="tpu_custom_call" | custom-call | tf_op jit(solution)/shard_map/pallas_call | solution.py:67
  19.0 95.3 %shard_map.74 = bf16[3,3,128,128]{3,2,1,0:T(8,128)(2,1)} custom-call(f32[3,2,4,4,4,3,32,128]{7,6,5,4,3,2,1,0:T(8,128)} %bitcast.4, bf16[2,3,128,128]{3,2,1,0:T(8,128)(2,1)} %bitcast.6, bf16[2,3,16,128,128]{4,3,2,1,0:T(8,128)(2,1)} %retarded.1, s32[3,2,16]{2,1,0:T(2,128)} %bitcast.7, f32[3,128,128]{2,1,0:T(8,128)} %inverse.1), custom_call_target="tpu_custom_call" | custom-call | tf_op jit(solution)/shard_map/pallas_call | solution.py:621
  114.3 1.7 %copy.9 = bf16[3,384,128]{2,1,0:T(8,128)(2,1)} copy(bf16[3,384,128]{2,1,0:T(8,128)(2,1)} %bitcast.5) | data formatting | bytes 589824

commit v6 on v5

--- a/solution.py
+++ b/solution.py
@@ -103,12 +103,14 @@
     return jnp.where(tiny, 0.0, CODES / jnp.where(tiny, 1.0, top)), jnp.where(tiny, 0.0, top * (1.0 / CODES))
 
 
+def coded(value):
+    there, back = scales_of(value)
+    return jnp.round(value * there).astype(jnp.int32).astype(CODE), jnp.squeeze(back, -2)
+
+
 def encode(source, codes, scales):
     def one(i, carry):
-        value = source[i]
-        there, back = scales_of(value)
-        codes[i] = jnp.round(value * there).astype(jnp.int32).astype(codes.dtype)
-        scales[i] = jnp.squeeze(back, -2)
+        codes[i], scales[i] = coded(source[i])
         return carry
 
     lax.fori_loop(0, source.shape[0], one, 0)
@@ -132,9 +134,9 @@
 def march_kernel(
     steps,
     part, own, retarded, columns, inverse, out,
-    gath, gath_young, ret, quad, peer, base, new, newer, sols, aside, hsum, hgot, ygot,
+    gath, gath_young, ret, quad, peer, base, new, newer, sols, aside, hsum, hout, hout_scale, hgot, hgot_scale, rgot, rgot_scale,
     zhalf, zhalf_scale, zfull, zfull_scale, zhalf_out, zhalf_out_scale, zfull_out, zfull_out_scale,
-    xgot, xgot_scale, xout, xout_scale,
+    pgot, pgot_scale, pout, pout_scale,
     send_sems, recv_sems, local_sems,
 ):
     panel, z = lax.axis_index("panel"), lax.axis_index("lag")
@@ -164,6 +166,31 @@
             device_id=to, device_id_type=MESH,
         )
 
+    class Bundle:
+        def __init__(self, pieces, got, sent=None):
+            i = used[0]
+            used[0] += 1
+
+            def make(src, dst, to):
+                return pltpu.make_async_remote_copy(
+                    src_ref=src, dst_ref=dst, send_sem=send_sems.at[i], recv_sem=recv_sems.at[i],
+                    device_id=to, device_id_type=MESH,
+                )
+
+            self.pieces = [make(*piece) for piece in pieces]
+            sent = got if sent is None else sent
+            self.got, self.sent = make(got, got, to_mate), make(sent, sent, to_mate)
+
+        def start(self):
+            for piece in self.pieces:
+                piece.start()
+
+        def wait_recv(self):
+            self.got.wait_recv()
+
+        def wait_send(self):
+            self.sent.wait_send()
+
     started = []
 
     def go(*copies):
@@ -186,10 +213,10 @@
             one.wait_recv()
 
     class Gather:
-        def __init__(self, view, go):
+        def __init__(self, view, side, go):
             whole = slice(None)
             self.go = go
-            self.first, self.pass_on, self.wide, self.wide_on, self.mates = [], [], [], [], []
+            self.first, self.pass_on, self.wide, self.wide_on, lines = [], [], [], [], []
             for half, (near, far) in enumerate(((to_x, to_y), (to_y, to_x))):
 
                 def spot(part, by, wide_by, half=half):
@@ -207,7 +234,8 @@
                 self.pass_on.append([sent(0, -1, 0, near[1]), sent(1, 1, 0, near[-1])])
                 self.wide.append({by: [sent(None, by, 0, far[d]) for d in (1, -1)] for by in (0, -1, 1, 2)})
                 self.wide_on.append({by: [sent(0, by, -1, far[1]), sent(1, by, 1, far[-1])] for by in (0, -1, 1, 2)})
-                self.mates.append([copy(line(by), line(by), to_mate) for by in (0, -1, 1, 2)])
+                lines += [(line(by), line(by), to_mate) for by in (0, -1, 1, 2)]
+            self.mates = Bundle(lines, side)
 
         def start(self):
             for half in (0, 1):
@@ -228,8 +256,7 @@
             for half in (0, 1):
                 landed(*self.pass_on[half])
                 self.go(*self.wide[half][2])
-            for half in (0, 1):
-                self.go(self.mates[half][0])
+            self.to_mates(0)
 
         def pass_wide(self, *which):
             for by in which:
@@ -246,26 +273,29 @@
 
         def pass_far(self):
             self.pass_wide(2)
-            for d in (0, 1):
-                for half in (0, 1):
-                    self.go(self.mates[half][1 + d])
+            self.to_mates(1, 2)
 
         def finish(self):
             for half in (0, 1):
                 for by in (0, -1, 1, 2):
                     landed(*self.wide_on[half][by])
-                self.go(self.mates[half][3])
-            for half in (0, 1):
-                landed(*self.mates[half])
+            self.to_mates(3)
+            landed(self.mates)
+
+        def to_mates(self, *which):
+            for i in which:
+                for half in (0, 1):
+                    self.mates.pieces[4 * half + i].start()
 
         def wait_sends(self):
             for half in (0, 1):
-                for group in (self.first, self.pass_on, self.mates, self.wide, self.wide_on):
+                for group in (self.first, self.pass_on, self.wide, self.wide_on):
                     members = group[half]
                     if isinstance(members, dict):
                         members = [one for pair in members.values() for one in pair]
                     for one in members:
                         one.wait_send()
+            self.mates.wait_send()
 
     def halves_of(buffer, *front):
         def view(half, part, yy, xx):
@@ -278,18 +308,18 @@
 
         return view
 
-    past = Gather(halves_of(gath, slice(None)), go)
+    past = Gather(halves_of(gath, slice(None)), gath.at[:, 0], only_start)
     between = used[0]
-    young = Gather(halves_of(gath_young, slice(None)), only_start)
+    young = Gather(halves_of(gath_young, slice(None)), gath_young.at[:, 0], only_start)
     used[0] = between
-    spread = [Gather(halves_of(new), only_start)]
+    spread = [Gather(halves_of(new), new.at[0], only_start)]
     used[0] = 0
-    spread.append(Gather(halves_of(newer), only_start))
+    spread.append(Gather(halves_of(newer), newer.at[0], only_start))
     used[0] = 2 * between
     younger = copy(own, gath_young.at[:, c, y, x], to_z[1])
 
     place, towards = {"z": z, "y": y, "x": x}, {"z": to_z, "y": to_y, "x": to_x}
-    orders = ["zxy"] * (steps - 1) + ["yxz"]
+    orders = ["zxy"] * steps
     ordered = (2, 1, -1, 0)
     whole = slice(None)
 
@@ -309,7 +339,8 @@
     def both(codes, scales, got, got_scales, to):
         return [copy(codes, got, to), copy(scales, got_scales, to)]
 
-    ring_far, ring_free, ring_tied, second_all, third_all = [], [], [], [], []
+    near_by = [(dy, dx) for dy in (0, *others) for dx in (0, *others) if (dy, dx) != (0, 0)]
+    ring_far, ring_free, ring_tied, over_plane = [], [], [], []
     for s, (first, then, last) in enumerate(orders):
         to = towards[first]
         ring_far.append([
@@ -326,18 +357,13 @@
 
         ring_free.append([near_half(i, 1 - i) for i in (0, 1)])
         ring_tied.append([near_half(i, i) for i in (0, 1)])
-        second_all.append([
-            both(xout.at[s, i], xout_scale.at[s, i], xgot.at[s, i], xgot_scale.at[s, i], towards[then][d])
-            for i, d in enumerate(others)
-        ])
-        third_all.append([
-            copy(
-                cut(quad, s, **{first: place[first], then: place[then], last: hop(place[last], d)}),
-                ygot.at[s, i], towards[last][d],
-            )
-            for i, d in enumerate(others)
-        ])
-
+        if first == "z":
+            codes, scales = [], []
+            for i, (dy, dx) in enumerate(near_by):
+                yy, xx = hop(y, dy), hop(x, dx)
+                codes.append((pout.at[s, yy, xx], pgot.at[s, i], (at(yy, xx, c), z)))
+                scales.append((pout_scale.at[s, yy, xx], pgot_scale.at[s, i], (at(yy, xx, c), z)))
+            over_plane.append([Bundle(codes, pgot.at[s]), Bundle(scales, pgot_scale.at[s])])
     def ring_part(s, by, h=None):
         first, _, last = orders[s]
         where = {first: hop(place[first], by)}
@@ -371,42 +397,53 @@
             add_decoded(ring_part(s, d, i), (zhalf.at[s, i], zhalf_scale.at[s, i]))
             send_near(s, i, i, ring_tied[s][i])
 
-    def to_second(s):
-        first, then, _ = orders[s]
+    def ring_end(s):
         for i in (0, 1):
             landed(*ring_free[s][i], *ring_tied[s][i])
         add_decoded(ring_part(s, 0), *((zfull.at[s, i], zfull_scale.at[s, i]) for i in (0, 1)))
-        for i, d in enumerate(others):
-            encode(cut(quad, s, **{first: place[first], then: hop(place[then], d)}), xout.at[s, i], xout_scale.at[s, i])
-            go(*second_all[s][i])
-
-    def to_third(s):
-        first, then, _ = orders[s]
-        for one in second_all[s]:
-            landed(*one)
-        mine = cut(quad, s, **{first: place[first], then: place[then]})
-        add_decoded(mine, *((xgot.at[s, i], xgot_scale.at[s, i]) for i in range(3)))
-        go(*third_all[s])
-
-    groups = [(s, 1) for s in range(steps)]
-    older = [
-        [
-            copy(hsum.at[pl.ds(first, n), :, hop(z, d)], hgot.at[i, pl.ds(first, n)], to_z[d])
-            for i, d in enumerate(others)
-        ]
-        for first, n in groups
+
+    def to_plane(s):
+        ring_end(s)
+        encode(quad.at[s, z], pout.at[s], pout_scale.at[s])
+        go(*over_plane[s])
+
+    def along_z(out, got, arrived):
+        return Bundle([(out(d), got(i), to_z[d]) for i, d in enumerate(others)], arrived)
+
+    older, right = [], []
+    for s in range(steps):
+        older.append([
+            along_z(lambda d, out=out: out.at[s, hop(z, d)], lambda i, got=got: got.at[s, i], got.at[s])
+            for out, got in ((hout, hgot), (hout_scale, hgot_scale))
+        ])
+        right.append([
+            along_z(lambda d, got=got: got.at[s, z], lambda i, got=got: got.at[s, z], got.at[s, pl.ds(0, 3)])
+            for got in (rgot, rgot_scale)
+        ])
+
+    def older_out(s):
+        hout[s], hout_scale[s] = coded(hsum[s])
+        go(*older[s])
+
+    def right_side(s):
+        total = quad[s, z, y, x] - hsum[s, z]
+        for i in range(3):
+            total = total - decode(hgot.at[s], hgot_scale.at[s], i)
+        landed(*over_plane[s])
+        for i in range(len(near_by)):
+            total = total + decode(pgot.at[s], pgot_scale.at[s], i)
+        rgot[s, z], rgot_scale[s, z] = coded(total)
+        go(*right[s])
+
+    def right_here(s):
+        landed(*right[s])
+        for q in range(RING):
+            base[s, :, q] = decode(rgot.at[s], rgot_scale.at[s], q)
+
+    told = [
+        Bundle([(sols.at[s, r], sols.at[s, r], to_z[d]) for r in range(own_blocks) for d in others], sols.at[s], sols)
+        for s in range(1, steps)
     ]
-    right = [[copy(base.at[s, :, z], base.at[s, :, z], to_z[d]) for d in others] for s in range(steps)]
-
-    def right_side(s):
-        landed(*third_all[s])
-        total = quad[s, z, y, x] - hsum[s, :, z]
-        for i in range(3):
-            total = total + (ygot[s, i] - hgot[i, s])
-        base[s, :, z] = total
-        go(*right[s])
-
-    told = {s: [[copy(sols.at[s, r], sols.at[s, r], to_z[d]) for r in range(own_blocks)] for d in others] for s in range(1, steps)}
 
     def field(buffer, front, col):
         chip = col // (2 * own_blocks)
@@ -422,20 +459,15 @@
             total = product if total is None else total + product
         return total
 
-    def older_sums(first, n):
+    def older_sums(s, which):
         def row(r, carry):
-            total = None
-            for lag in range(lags):
-
-                def fields(col, lag=lag):
-                    entries = [lag - s for s in range(first, first + n)]
-                    found = [field(gath, (e,), col) if e >= 0 else field(gath_young, (lags + e,), col) for e in entries]
-                    return jnp.concatenate(found, 1)
-
-                value = pairs(lag, r, fields)
+            total = None if which[-1] == lags - 1 else hsum[s, :, r].reshape(width, width)
+            for lag in which:
+                e = lag - s
+                entry, buffer = (e, gath) if e >= 0 else (lags + e, gath_young)
+                value = pairs(lag, r, lambda col, entry=entry, buffer=buffer: field(buffer, (entry,), col))
                 total = value if total is None else total + value
-            for j in range(n):
-                hsum[first + j, r] = total[:, j * width : (j + 1) * width].reshape(RING, quarter, width)
+            hsum[s, :, r] = total.reshape(RING, quarter, width)
             return carry
 
         lax.fori_loop(0, own_blocks, row, 0)
@@ -470,7 +502,7 @@
         pl.when(z > 0)(act)
 
     barrier = pltpu.get_barrier_semaphore()
-    neighbours = [*to_x.values(), *to_y.values(), *to_z.values(), to_mate]
+    neighbours = [(at(hop(y, dy), hop(x, dx), c), z) for dy, dx in near_by] + [*to_z.values(), to_mate]
     for to in neighbours:
         pl.semaphore_signal(barrier, inc=1, device_id=to, device_id_type=MESH)
     for pieces in kept:
@@ -508,25 +540,23 @@
     past.pass_near()
     past.pass_far()
     following(start_young)
-    to_second(0)
+    to_plane(0)
     matrices.wait()
     past.finish()
-    leading(lambda: over_cores(2, ordered[:1]))
-    older_sums(*groups[0])
-    go(*older[0])
+    older_sums(0, range(lags))
+    older_out(0)
     following(young.pass_chunks)
-    to_third(0)
-    leading(lambda: over_cores(2, ordered[1:]))
+    older_sums(1, range(1, lags))
+    landed(*older[0])
+    right_side(0)
+    ring_pass(1)
     following(young.far_chunk)
-    landed(*older[0])
-    ring_pass(1)
-    right_side(0)
     following(young.pass_own)
     following(young.pass_near)
-    leading(lambda: ring_pass(2))
+    old = len(started)
+    over_cores(2)
     following(young.pass_far)
-    to_second(1)
-    landed(*right[0])
+    right_here(0)
     solve(0)
 
     def send_first():
@@ -534,68 +564,56 @@
         spread[0].start()
 
     leading(send_first)
-    following(lambda: over_cores(2))
+    leading(spread[0].pass_chunks)
+    to_plane(1)
     following(young.finish)
-    older_sums(*groups[1])
-    go(*older[1])
-    leading(spread[0].pass_chunks)
-    to_third(1)
+    older_sums(1, range(1))
+    older_out(1)
     leading(spread[0].far_chunk)
+    ring_pass(2)
+    older_sums(2, range(lags))
     landed(*older[1])
+    right_side(1)
+    older_out(2)
     leading(spread[0].pass_own)
     leading(spread[0].pass_near)
-    old = len(started)
-    right_side(1)
-    following(lambda: ring_pass(2))
     leading(spread[0].pass_far)
-    leading(lambda: to_second(2))
-    older_sums(*groups[2])
     drain(old)
-    landed(*right[1])
+    past.wait_sends()
+    to_plane(2)
+    right_here(1)
 
     def second():
         spread[0].finish()
         solve(1, new)
         newer[c, y, x] = sols[1]
         spread[1].start()
-        for pieces in told[1]:
-            only_start(*pieces)
+        told[0].start()
 
     leading(second)
-    go(*older[2])
-    following(lambda: to_second(2))
     leading(lambda: set_aside(1, new))
-    to_third(2)
     leading(spread[1].pass_chunks)
     leading(spread[1].far_chunk)
     landed(*older[2])
     leading(spread[0].wait_sends)
     leading(spread[1].pass_own)
     leading(spread[1].pass_near)
+    leading(spread[1].pass_far)
     right_side(2)
-    leading(spread[1].pass_far)
-    landed(*right[2])
+    right_here(2)
 
     def third():
         spread[1].finish()
         for r in range(own_blocks):
             solve_row(2, r, newer)
-            only_start(*(pieces[r] for pieces in told[2]))
+            only_start(*told[1].pieces[3 * r : 3 * r + 3])
         spread[1].wait_sends()
-        for s in range(1, steps):
-            for pieces in told[s]:
-                for one in pieces:
-                    one.wait_send()
+        for one in told:
+            one.wait_send()
 
     leading(third)
 
-    for i, d in enumerate(others):
-
-        @pl.when(z == d % RING)
-        def take(i=i):
-            for s in range(1, steps):
-                landed(*told[s][i])
-
+    following(lambda: landed(*told))
     pl.when(z < RING - 1)(younger.wait_send)
     following(young.wait_sends)
     for one in started:
@@ -612,12 +630,12 @@
     line = (own_blocks, cases)
     bf16 = own.dtype
     plane = (2, RING, RING, own_blocks, width, cases)
-    halves, fulls, direct = (steps, 2, RING // 2, RING), (steps, 2, RING, RING), (steps, 3, RING)
-
-    def coded(lead):
+    halves, fulls = (steps, 2, RING // 2, RING), (steps, 2, RING, RING)
+
+    def parcels(lead):
         return [pltpu.VMEM((*lead, *piece), CODE), pltpu.VMEM((*lead, *line), SUM)]
 
-    copies = 208
+    copies = 151
     return pl.pallas_call(
         functools.partial(march_kernel, steps),
         out_shape=jax.ShapeDtypeStruct((steps, own_blocks, width, cases), bf16),
@@ -640,11 +658,10 @@
             pltpu.VMEM(plane, bf16),
             pltpu.VMEM((steps, own_blocks, width, cases), bf16),
             pltpu.VMEM((own_blocks, width, cases), SUM),
-            pltpu.VMEM((steps, own_blocks, RING, quarter, cases), SUM),
-            pltpu.VMEM((3, steps, *piece), SUM),
-            pltpu.VMEM((steps, 3, *piece), SUM),
-            *coded(halves), *coded(fulls), *coded(halves), *coded(fulls),
-            *coded(direct), *coded(direct),
+            pltpu.VMEM((steps, RING, *piece), SUM),
+            *parcels((steps, RING)), *parcels((steps, 3)), *parcels((steps, RING)),
+            *parcels(halves), *parcels(fulls), *parcels(halves), *parcels(fulls),
+            *parcels((steps, RING * RING - 1)), *parcels((steps, RING, RING)),
             pltpu.SemaphoreType.DMA((copies,)),
             pltpu.SemaphoreType.DMA((copies,)),
             pltpu.SemaphoreType.DMA((steps + 1, RING)),

time: 117 us -> 114 us (0.974)
  Pallas kernels: 114 us -> 111 us
    pallas_call x1, Pallas kernels: 95.3 us -> 92.4 us  [march(): pl.pallas_call(functools.partial(march_kernel, steps), out_shape=jax.Shap...]
where the time goes in v6:
time: 114 us; the launch traced here: 113 us
  Pallas kernels  111 us (97%)
  local copies, waits for them, and re-layouts  1.69 us (1%)
    pallas_call x1, Pallas kernels, march(): pl.pallas_call(functools.partial(march_kernel, steps), out_shape=jax.Shap...  92.4 us
    pallas_call x1, Pallas kernels, incident_partial(): pl.pallas_call(functools.partial(incident_kernel, per_cell, steps), out_s...  19 us

profile of v6, /device:TPU:65, one launch (start us, length us, event | category | flops | bytes accessed | tf_op | source)
XLA Modules:
  0.0 113.1 jit_solution(17136373516197813306)
XLA Ops:
  0.0 19.0 %shard_map.73 = f32[3,2,4,16,3,32,128]{6,5,4,3,2,1,0:T(8,128)} custom-call(s32[256]{0:T(256)} %targets.1, bf16[256,128,128]{2,1,0:T(8,128)(2,1)} %green.1, bf16[1024,384]{1,0:T(8,128)(2,1)} %cells.1), custom_call_target="tpu_custom_call" | custom-call | tf_op jit(solution)/shard_map/pallas_call | solution.py:67
  19.0 92.4 %shard_map.74 = bf16[3,3,128,128]{3,2,1,0:T(8,128)(2,1)} custom-call(f32[3,2,4,4,4,3,32,128]{7,6,5,4,3,2,1,0:T(8,128)} %bitcast.4, bf16[2,3,128,128]{3,2,1,0:T(8,128)(2,1)} %bitcast.6, bf16[2,3,16,128,128]{4,3,2,1,0:T(8,128)(2,1)} %retarded.1, s32[3,2,16]{2,1,0:T(2,128)} %bitcast.7, f32[3,128,128]{2,1,0:T(8,128)} %inverse.1), custom_call_target="tpu_custom_call" | custom-call | tf_op jit(solution)/shard_map/pallas_call | solution.py:639
  111.4 1.7 %copy.9 = bf16[3,384,128]{2,1,0:T(8,128)(2,1)} copy(bf16[3,384,128]{2,1,0:T(8,128)(2,1)} %bitcast.5) | data formatting | bytes 589824

commit v7 on v6

--- a/solution.py
+++ b/solution.py
@@ -515,8 +515,6 @@
     go(*cores[0])
     past.start()
     pl.when(z < RING - 1)(younger.start)
-    for pieces in cores[1:]:
-        go(*pieces)
 
     def nothing_younger():
         def clear(i, carry):
@@ -532,11 +530,13 @@
         young.start()
 
     over_cores(0)
+    go(*cores[1])
     past.pass_chunks()
     past.far_chunk()
     ring_pass(0)
     past.pass_own()
     over_cores(1)
+    go(*cores[2])
     past.pass_near()
     past.pass_far()
     following(start_young)

time: 114 us -> 114 us (level)
  no operation moved by 1% of the time
where the time goes in v7:
time: 114 us; the launch traced here: 113 us
  Pallas kernels  111 us (97%)
  local copies, waits for them, and re-layouts  1.69 us (1%)
    pallas_call x1, Pallas kernels, march(): pl.pallas_call(functools.partial(march_kernel, steps), out_shape=jax.Shap...  92.4 us
    pallas_call x1, Pallas kernels, incident_partial(): pl.pallas_call(functools.partial(incident_kernel, per_cell, steps), out_s...  19 us

profile of v7, /device:TPU:65, one launch (start us, length us, event | category | flops | bytes accessed | tf_op | source)
XLA Modules:
  0.0 113.1 jit_solution(6803772995690933069)
XLA Ops:
  0.0 19.0 %shard_map.73 = f32[3,2,4,16,3,32,128]{6,5,4,3,2,1,0:T(8,128)} custom-call(s32[256]{0:T(256)} %targets.1, bf16[256,128,128]{2,1,0:T(8,128)(2,1)} %green.1, bf16[1024,384]{1,0:T(8,128)(2,1)} %cells.1), custom_call_target="tpu_custom_call" | custom-call | tf_op jit(solution)/shard_map/pallas_call | solution.py:67
  19.0 92.4 %shard_map.74 = bf16[3,3,128,128]{3,2,1,0:T(8,128)(2,1)} custom-call(f32[3,2,4,4,4,3,32,128]{7,6,5,4,3,2,1,0:T(8,128)} %bitcast.4, bf16[2,3,128,128]{3,2,1,0:T(8,128)(2,1)} %bitcast.6, bf16[2,3,16,128,128]{4,3,2,1,0:T(8,128)(2,1)} %retarded.1, s32[3,2,16]{2,1,0:T(2,128)} %bitcast.7, f32[3,128,128]{2,1,0:T(8,128)} %inverse.1), custom_call_target="tpu_custom_call" | custom-call | tf_op jit(solution)/shard_map/pallas_call | solution.py:639
  111.4 1.7 %copy.9 = bf16[3,384,128]{2,1,0:T(8,128)(2,1)} copy(bf16[3,384,128]{2,1,0:T(8,128)(2,1)} %bitcast.5) | data formatting | bytes 589824

commit v8 on v6

--- a/solution.py
+++ b/solution.py
@@ -213,10 +213,10 @@
             one.wait_recv()
 
     class Gather:
-        def __init__(self, view, side, go):
+        def __init__(self, view, side, row, go):
             whole = slice(None)
             self.go = go
-            self.first, self.pass_on, self.wide, self.wide_on, lines = [], [], [], [], []
+            self.first, self.pass_on, self.wide, lines, onward = [], [], [], [], []
             for half, (near, far) in enumerate(((to_x, to_y), (to_y, to_x))):
 
                 def spot(part, by, wide_by, half=half):
@@ -233,9 +233,11 @@
                 self.first.append([sent(None, 0, 0, near[d]) for d in (1, -1)])
                 self.pass_on.append([sent(0, -1, 0, near[1]), sent(1, 1, 0, near[-1])])
                 self.wide.append({by: [sent(None, by, 0, far[d]) for d in (1, -1)] for by in (0, -1, 1, 2)})
-                self.wide_on.append({by: [sent(0, by, -1, far[1]), sent(1, by, 1, far[-1])] for by in (0, -1, 1, 2)})
+                for by in (0, -1, 1, 2):
+                    onward += [(spot(i, by, d), spot(i, by, d), far[-d]) for i, d in enumerate((-1, 1))]
                 lines += [(line(by), line(by), to_mate) for by in (0, -1, 1, 2)]
             self.mates = Bundle(lines, side)
+            self.wide_on = Bundle(onward, row)
 
         def start(self):
             for half in (0, 1):
@@ -263,7 +265,7 @@
                 for d in (0, 1):
                     for half in (0, 1):
                         landed(self.wide[half][by][d])
-                        self.go(self.wide_on[half][by][d])
+                        self.wide_on.pieces[8 * half + 2 * (0, -1, 1, 2).index(by) + d].start()
 
         def pass_own(self):
             self.pass_wide(0)
@@ -276,9 +278,7 @@
             self.to_mates(1, 2)
 
         def finish(self):
-            for half in (0, 1):
-                for by in (0, -1, 1, 2):
-                    landed(*self.wide_on[half][by])
+            landed(self.wide_on)
             self.to_mates(3)
             landed(self.mates)
 
@@ -289,12 +289,13 @@
 
         def wait_sends(self):
             for half in (0, 1):
-                for group in (self.first, self.pass_on, self.wide, self.wide_on):
+                for group in (self.first, self.pass_on, self.wide):
                     members = group[half]
                     if isinstance(members, dict):
                         members = [one for pair in members.values() for one in pair]
                     for one in members:
                         one.wait_send()
+            self.wide_on.wait_send()
             self.mates.wait_send()
 
     def halves_of(buffer, *front):
@@ -308,13 +309,13 @@
 
         return view
 
-    past = Gather(halves_of(gath, slice(None)), gath.at[:, 0], only_start)
+    past = Gather(halves_of(gath, slice(None)), gath.at[:, 0], gath.at[:, 0, 0], only_start)
     between = used[0]
-    young = Gather(halves_of(gath_young, slice(None)), gath_young.at[:, 0], only_start)
+    young = Gather(halves_of(gath_young, slice(None)), gath_young.at[:, 0], gath_young.at[:, 0, 0], only_start)
     used[0] = between
-    spread = [Gather(halves_of(new), new.at[0], only_start)]
+    spread = [Gather(halves_of(new), new.at[0], new.at[0, 0], only_start)]
     used[0] = 0
-    spread.append(Gather(halves_of(newer), newer.at[0], only_start))
+    spread.append(Gather(halves_of(newer), newer.at[0], newer.at[0, 0], only_start))
     used[0] = 2 * between
     younger = copy(own, gath_young.at[:, c, y, x], to_z[1])
 
@@ -340,7 +341,7 @@
         return [copy(codes, got, to), copy(scales, got_scales, to)]
 
     near_by = [(dy, dx) for dy in (0, *others) for dx in (0, *others) if (dy, dx) != (0, 0)]
-    ring_far, ring_free, ring_tied, over_plane = [], [], [], []
+    ring_far, ring_near, over_plane = [], [], []
     for s, (first, then, last) in enumerate(orders):
         to = towards[first]
         ring_far.append([
@@ -348,15 +349,11 @@
             for i, d in enumerate((1, -1))
         ])
 
-        def near_half(i, h, s=s, to=to):
-            rows = pl.ds(2 * h, 2)
-            return both(
-                zfull_out.at[s, i, rows], zfull_out_scale.at[s, i, rows], zfull.at[s, i, rows],
-                zfull_scale.at[s, i, rows], to[(1, -1)[i]],
-            )
-
-        ring_free.append([near_half(i, 1 - i) for i in (0, 1)])
-        ring_tied.append([near_half(i, i) for i in (0, 1)])
+        near = [(i, pl.ds(2 * h, 2), to[d]) for i, d in enumerate((1, -1)) for h in (0, 1)]
+        ring_near.append([
+            Bundle([(out.at[s, i, rows], got.at[s, i, rows], there) for i, rows, there in near], got.at[s])
+            for out, got in ((zfull_out, zfull), (zfull_out_scale, zfull_scale))
+        ])
         if first == "z":
             codes, scales = [], []
             for i, (dy, dx) in enumerate(near_by):
@@ -371,10 +368,10 @@
             where[last] = pl.ds(2 * h, 2)
         return cut(quad, s, **where)
 
-    def send_near(s, i, h, copies):
+    def send_near(s, i, h):
         rows = pl.ds(2 * h, 2)
         encode(ring_part(s, (1, -1)[i], h), zfull_out.at[s, i, rows], zfull_out_scale.at[s, i, rows])
-        go(*copies)
+        only_start(*(bundle.pieces[2 * i + h] for bundle in ring_near[s]))
 
     def over_cores(s, which=ordered):
         first = orders[s][0]
@@ -389,17 +386,17 @@
                     go(*ring_far[s][i])
             elif by:
                 i = (1, -1).index(by)
-                send_near(s, i, 1 - i, ring_free[s][i])
+                send_near(s, i, 1 - i)
 
     def ring_pass(s):
         for i, d in enumerate((1, -1)):
             landed(*ring_far[s][i])
             add_decoded(ring_part(s, d, i), (zhalf.at[s, i], zhalf_scale.at[s, i]))
-            send_near(s, i, i, ring_tied[s][i])
+            send_near(s, i, i)
+        started.extend(ring_near[s])
 
     def ring_end(s):
-        for i in (0, 1):
-            landed(*ring_free[s][i], *ring_tied[s][i])
+        landed(*ring_near[s])
         add_decoded(ring_part(s, 0), *((zfull.at[s, i], zfull_scale.at[s, i]) for i in (0, 1)))
 
     def to_plane(s):
@@ -635,7 +632,7 @@
     def parcels(lead):
         return [pltpu.VMEM((*lead, *piece), CODE), pltpu.VMEM((*lead, *line), SUM)]
 
-    copies = 151
+    copies = 103
     return pl.pallas_call(
         functools.partial(march_kernel, steps),
         out_shape=jax.ShapeDtypeStruct((steps, own_blocks, width, cases), bf16),

time: 114 us -> 114 us (level)
  no operation moved by 1% of the time
where the time goes in v8:
time: 114 us; the launch traced here: 112 us
  Pallas kernels  111 us (97%)
  local copies, waits for them, and re-layouts  1.69 us (1%)
    pallas_call x1, Pallas kernels, march(): pl.pallas_call(functools.partial(march_kernel, steps), out_shape=jax.Shap...  91.5 us
    pallas_call x1, Pallas kernels, incident_partial(): pl.pallas_call(functools.partial(incident_kernel, per_cell, steps), out_s...  19 us

profile of v8, /device:TPU:65, one launch (start us, length us, event | category | flops | bytes accessed | tf_op | source)
XLA Modules:
  0.0 112.2 jit_solution(7901671015192462750)
XLA Ops:
  0.0 19.0 %shard_map.73 = f32[3,2,4,16,3,32,128]{6,5,4,3,2,1,0:T(8,128)} custom-call(s32[256]{0:T(256)} %targets.1, bf16[256,128,128]{2,1,0:T(8,128)(2,1)} %green.1, bf16[1024,384]{1,0:T(8,128)(2,1)} %cells.1), custom_call_target="tpu_custom_call" | custom-call | tf_op jit(solution)/shard_map/pallas_call | solution.py:67
  19.0 91.5 %shard_map.74 = bf16[3,3,128,128]{3,2,1,0:T(8,128)(2,1)} custom-call(f32[3,2,4,4,4,3,32,128]{7,6,5,4,3,2,1,0:T(8,128)} %bitcast.4, bf16[2,3,128,128]{3,2,1,0:T(8,128)(2,1)} %bitcast.6, bf16[2,3,16,128,128]{4,3,2,1,0:T(8,128)(2,1)} %retarded.1, s32[3,2,16]{2,1,0:T(2,128)} %bitcast.7, f32[3,128,128]{2,1,0:T(8,128)} %inverse.1), custom_call_target="tpu_custom_call" | custom-call | tf_op jit(solution)/shard_map/pallas_call | solution.py:636
  110.5 1.7 %copy.9 = bf16[3,384,128]{2,1,0:T(8,128)(2,1)} copy(bf16[3,384,128]{2,1,0:T(8,128)(2,1)} %bitcast.5) | data formatting | bytes 589824
